TPU v7x, 32 devices: a whole 2x2x4 slice. The times are simulated.
32 devices in a mesh: expert: 4 (over y, x), dp: 8 (over z, core).
Axes of the slice: x: 2, y: 2, z: 4, core: 2. Of those that a mesh axis runs over, the one named last changes fastest.
Arguments:
- tokens_in: bfloat16 [16384, 768], P(('expert', 'dp')), may hold values from -6 to 6
- segment_ids: int32 [32, 512], P(('expert', 'dp')), may hold values from 0 to 7, never falling along the last dimension, each value on 1 to 256 neighbouring positions
- expert_index: int32 [16384], P(('expert', 'dp')), may hold values from 0 to 3, as said below
- expert_slot: int32 [16384], P(('expert', 'dp')), may hold values from 0 to 191, as said below
- attn_gain: bfloat16 [2, 768], P(None, ('expert', 'dp')), may hold values from 0.099609375 to 1.8984375
- qkv_weight: bfloat16 [768, 2, 2304], P(('expert', 'dp')), may hold values from -0.21875 to 0.21875
- out_weight: bfloat16 [768, 2, 768], P(('expert', 'dp')), may hold values from -1.75 to 1.75
- rel_bias: float32 [32, 12], replicated, may hold values from -4 to 4
- ffn_gain: bfloat16 [2, 768], P(None, ('expert', 'dp')), may hold values from 0.099609375 to 1.8984375
- ffn_in: bfloat16 [768, 3072], P(('expert', 'dp')), may hold values from -0.21875 to 0.21875
- ffn_out: bfloat16 [3072, 768], P(('expert', 'dp')), may hold values from -0.109375 to 0.109375
- router: bfloat16 [768, 4], P(('expert', 'dp')), may hold values from -0.14941406 to 0.14941406
- expert_in: bfloat16 [4, 768, 3072], P('expert', 'dp'), may hold values from -0.21875 to 0.21875
- expert_out: bfloat16 [4, 3072, 768], P('expert', 'dp'), may hold values from -0.875 to 0.875
- cotangent: bfloat16 [16384, 768], P(('expert', 'dp')), may hold values from -6 to 6
Outputs:
- tokens_out: bfloat16 [16384, 768], P(('expert', 'dp'))
- tokens_grad: float32 [16384, 768], P(('expert', 'dp'))
- attn_gain_grad: float32 [2, 768], P(None, ('expert', 'dp'))
- qkv_weight_grad: float32 [768, 2, 2304], P(('expert', 'dp'))
- out_weight_grad: float32 [768, 2, 768], P(('expert', 'dp'))
- rel_bias_grad: float32 [32, 12], replicated
- ffn_gain_grad: float32 [2, 768], P(None, ('expert', 'dp'))
- ffn_in_grad: float32 [768, 3072], P(('expert', 'dp'))
- ffn_out_grad: float32 [3072, 768], P(('expert', 'dp'))
- router_grad: float32 [768, 4], P(('expert', 'dp'))
- expert_in_grad: float32 [4, 768, 3072], P('expert', 'dp')
- expert_out_grad: float32 [4, 3072, 768], P('expert', 'dp')
Inputs may be any that keep to these rules, and one draw needn't show every extreme that they name: `expert_index`: in every draw one expert is named by 128 + 64 tokens of every device; every other expert by at most 128 tokens of one device. `expert_slot`: the tokens of one device that name one expert hold distinct slots; a slot of 128 or more drops the token. The busiest expert's tokens of every device hold the slots 0 to 191; the others' slots are below 128.
All inputs are finite; a program needn't handle non-finite values.
Results may differ from a plain program's by a relative error of at most 0.024.
Values may be sent and summed in bfloat16 or wider, within the bound.
No kernel may reach another device: no remote copies, remote signals or barrier semaphores. Data moves between devices by JAX's collectives and lax.ppermute only.
A program may use at most 256 MiB of HBM per device.

v0:
```python
import jax
import jax.numpy as jnp
from jax import lax
from jax.sharding import PartitionSpec as P

HEADS = 12
DH = 64
BUCKETS = 32
SEQ = 512


EPSILON = 1e-06
NEG_FILL = -1e30
PRECISE = lax.Precision.HIGHEST


def bucket_of(offset):
    distance = jnp.abs(offset)
    far_bucket = jnp.full_like(distance, 8)
    for level_id in range(1, 8):
        far_bucket = far_bucket + (distance * distance >= 64 * 2**level_id).astype(jnp.int32)
    near_bucket = jnp.where(distance < 8, distance, far_bucket)
    return near_bucket + 16 * (offset > 0).astype(jnp.int32)


def pair_onehot():
    offsets = jnp.arange(SEQ, dtype=jnp.int32)[None, :] - jnp.arange(SEQ, dtype=jnp.int32)[:, None]
    return (
        bucket_of(offsets)[:, :, None] == jnp.arange(BUCKETS, dtype=jnp.int32)[None, None, :]
    ).astype(jnp.float32)


def norm_scale(stream, gain_row):
    inverse = lax.rsqrt(jnp.mean(stream * stream, axis=-1, keepdims=True) + EPSILON)
    return stream * inverse * gain_row


def norm_backward(grad_normed, stream, gain_row):
    normed_again, norm_pull = jax.vjp(norm_scale, stream, gain_row.astype(jnp.float32))
    grad_input, grad_gain = norm_pull(grad_normed)
    return (grad_input, grad_gain)


def gelu_tanh(value):
    return jax.nn.gelu(value, approximate=True)


def gate_of(logits, chosen):
    return jnp.sum(jax.nn.softmax(logits, axis=-1) * chosen, axis=-1)


def split_heads(packed):
    token_count = packed.shape[0]
    model_width = packed.shape[1] // 3
    query_all = packed[:, :model_width].reshape(token_count, HEADS, DH)
    key_all = packed[:, model_width : 2 * model_width].reshape(token_count, HEADS, DH)
    value_all = packed[:, 2 * model_width :].reshape(token_count, HEADS, DH)
    return (query_all, key_all, value_all)


def block_layout(token_count):
    block_rows = min(512, SEQ)
    return (block_rows, token_count // block_rows, SEQ // block_rows)


def block_scores(query_rows, key_rows, query_segs, key_segs, bias_full):
    raw_scores = jnp.einsum(
        "qhd,khd->hqk", query_rows, key_rows, preferred_element_type=jnp.float32
    )
    allowed = (query_segs[:, None] == key_segs[None, :])[None]
    return jnp.where(allowed, raw_scores * DH ** (-0.5) + bias_full, NEG_FILL)


def attend_forward(packed, segments, bias_full):
    query_all, key_all, value_all = split_heads(packed)
    seg_flat = segments.reshape(-1)
    token_count = packed.shape[0]
    block_rows, block_count, per_sequence = block_layout(token_count)

    def one_block(block_id):
        scores = block_scores(query_all, key_all, seg_flat, seg_flat, bias_full)
        top_score = jnp.max(scores, axis=-1, keepdims=True)
        exp_scores = jnp.exp(scores - top_score)
        totals = jnp.sum(exp_scores, axis=-1, keepdims=True)
        prob_low = (exp_scores / totals).astype(jnp.bfloat16)
        mixed_rows = jnp.einsum(
            "hqk,khd->qhd", prob_low, value_all, preferred_element_type=jnp.float32
        )
        return (
            mixed_rows.astype(jnp.bfloat16).reshape(block_rows, -1),
            (top_score + jnp.log(totals))[:, :, 0],
        )

    mixed_all, log_totals = lax.map(one_block, jnp.arange(block_count, dtype=jnp.int32))
    return (mixed_all.reshape(token_count, -1), log_totals)


def attend_backward(packed, segments, bias_full, log_totals, grad_mixed):
    query_all, key_all, value_all = split_heads(packed)
    seg_flat = segments.reshape(-1)
    token_count = packed.shape[0]
    block_rows, block_count, per_sequence = block_layout(token_count)
    grad_heads = grad_mixed.reshape(token_count, HEADS, DH)

    def one_block(running, block_id):
        grad_keys, grad_values, grad_pairs = running
        scores = block_scores(query_all, key_all, seg_flat, seg_flat, bias_full)
        weights_now = jnp.exp(scores - log_totals[block_id][:, :, None])
        grad_weights = jnp.einsum(
            "qhd,khd->hqk", grad_heads, value_all, preferred_element_type=jnp.float32
        )
        grad_scores = weights_now * (
            grad_weights - jnp.sum(weights_now * grad_weights, axis=-1, keepdims=True)
        )
        grad_pairs = grad_pairs + grad_scores
        grad_raw = (grad_scores * DH ** (-0.5)).astype(jnp.bfloat16)
        grad_query = jnp.einsum(
            "hqk,khd->qhd", grad_raw, key_all, preferred_element_type=jnp.float32
        )
        key_part = jnp.einsum(
            "hqk,qhd->khd", grad_raw, query_all, preferred_element_type=jnp.float32
        )
        value_part = jnp.einsum(
            "hqk,qhd->khd",
            weights_now.astype(jnp.bfloat16),
            grad_heads,
            preferred_element_type=jnp.float32,
        )
        grad_keys = grad_keys + key_part
        grad_values = grad_values + value_part
        return ((grad_keys, grad_values, grad_pairs), grad_query.reshape(block_rows, -1))

    zero_heads = jnp.zeros((token_count, HEADS, DH), jnp.float32)
    zero_pairs = jnp.zeros((HEADS, SEQ, SEQ), jnp.float32)
    finished, grad_query_all = lax.scan(
        one_block, (zero_heads, zero_heads, zero_pairs), jnp.arange(block_count, dtype=jnp.int32)
    )
    grad_packed = jnp.concatenate(
        [
            grad_query_all.reshape(token_count, -1),
            finished[0].reshape(token_count, -1),
            finished[1].reshape(token_count, -1),
        ],
        axis=1,
    )
    return (grad_packed, finished[2])


def attention_forward(stream, gain_row, qkv_full, out_full, segments, bias_full):
    normed_low = norm_scale(stream, gain_row.astype(jnp.float32)).astype(jnp.bfloat16)
    packed_low = jnp.dot(normed_low, qkv_full, preferred_element_type=jnp.float32).astype(
        jnp.bfloat16
    )
    mixed_low, log_totals = attend_forward(packed_low, segments, bias_full)
    stream_after = stream + jnp.dot(mixed_low, out_full, preferred_element_type=jnp.float32)
    return (normed_low, packed_low, mixed_low, log_totals, stream_after)


def attention_backward(
    grad_stream, stream, gain_row, qkv_full, out_full, segments, bias_full, kept_state
):
    normed_low = kept_state[0]
    packed_low = kept_state[1]
    mixed_low = kept_state[2]
    log_totals = kept_state[3]
    grad_low = grad_stream.astype(jnp.bfloat16)
    grad_out_w = jnp.einsum("td,te->de", mixed_low, grad_low, preferred_element_type=jnp.float32)
    grad_mixed = jnp.einsum(
        "te,de->td", grad_low, out_full, preferred_element_type=jnp.float32
    ).astype(jnp.bfloat16)
    grad_packed, grad_pairs = attend_backward(
        packed_low, segments, bias_full, log_totals, grad_mixed
    )
    packed_grad_low = grad_packed.astype(jnp.bfloat16)
    grad_qkv_w = jnp.einsum(
        "td,te->de", normed_low, packed_grad_low, preferred_element_type=jnp.float32
    )
    grad_normed = jnp.einsum(
        "te,de->td", packed_grad_low, qkv_full, preferred_element_type=jnp.float32
    )
    grad_input, grad_gain = norm_backward(grad_normed, stream, gain_row)
    return (grad_stream + grad_input, grad_gain, grad_qkv_w, grad_out_w, grad_pairs)


def dense_forward(stream, gain_row, weight_in, weight_out):
    normed_low = norm_scale(stream, gain_row.astype(jnp.float32)).astype(jnp.bfloat16)
    hidden_pre = jnp.dot(normed_low, weight_in, preferred_element_type=jnp.float32)
    hidden_low = gelu_tanh(hidden_pre).astype(jnp.bfloat16)
    stream_after = stream + jnp.dot(hidden_low, weight_out, preferred_element_type=jnp.float32)
    return (normed_low, hidden_pre, stream_after)


def dense_backward(grad_stream, stream, gain_row, weight_in, weight_out, kept_state):
    normed_low = kept_state[0]
    hidden_pre = kept_state[1]
    grad_low = grad_stream.astype(jnp.bfloat16)
    gelu_value, gelu_pull = jax.vjp(gelu_tanh, hidden_pre)
    hidden_low = gelu_value.astype(jnp.bfloat16)
    grad_w_out = jnp.einsum("tf,td->fd", hidden_low, grad_low, preferred_element_type=jnp.float32)
    grad_hidden = (
        jnp.einsum("td,fd->tf", grad_low, weight_out, preferred_element_type=jnp.float32)
        .astype(jnp.bfloat16)
        .astype(jnp.float32)
    )
    grad_pre = gelu_pull(grad_hidden)[0].astype(jnp.bfloat16)
    grad_w_in = jnp.einsum("td,tf->df", normed_low, grad_pre, preferred_element_type=jnp.float32)
    grad_normed = jnp.einsum("tf,df->td", grad_pre, weight_in, preferred_element_type=jnp.float32)
    grad_input, grad_gain = norm_backward(grad_normed, stream, gain_row)
    return (grad_stream + grad_input, grad_gain, grad_w_in, grad_w_out)


def dispatch_table(expert_ids, slot_ids, expert_count, capacity):
    target = jnp.where(slot_ids < capacity, expert_ids * capacity + slot_ids, -1)
    return (
        target[:, None] == jnp.arange(expert_count * capacity, dtype=jnp.int32)[None, :]
    ).astype(jnp.bfloat16)


def expert_forward(received, weight_in, weight_out):
    hidden_pre = jnp.einsum(
        "secd,edf->secf", received, weight_in, preferred_element_type=jnp.float32
    )
    hidden_low = gelu_tanh(hidden_pre).astype(jnp.bfloat16)
    produced = jnp.einsum(
        "secf,efd->secd", hidden_low, weight_out, preferred_element_type=jnp.float32
    )
    return (produced.astype(jnp.bfloat16), hidden_pre, received)


def sparse_forward(
    stream, gain_row, router_full, in_full, out_experts, expert_ids, slot_ids, expert_count
):
    normed_low = norm_scale(stream, gain_row.astype(jnp.float32)).astype(jnp.bfloat16)
    logits = jnp.dot(normed_low, router_full, preferred_element_type=jnp.float32)
    chosen = (expert_ids[:, None] == jnp.arange(expert_count, dtype=jnp.int32)[None, :]).astype(
        jnp.float32
    )
    gate_values = gate_of(logits, chosen)
    capacity = stream.shape[0] // expert_count
    slot_table = dispatch_table(expert_ids, slot_ids, expert_count, capacity)
    outgoing = jnp.einsum(
        "ts,td->sd", slot_table, normed_low, preferred_element_type=jnp.float32
    ).astype(jnp.bfloat16)
    outgoing = outgoing.reshape(expert_count // in_full.shape[0], in_full.shape[0], capacity, -1)
    produced, hidden_pre, received = expert_forward(
        lax.all_to_all(outgoing, "expert", split_axis=0, concat_axis=0, tiled=True),
        in_full,
        out_experts,
    )
    returned = lax.all_to_all(produced, "expert", split_axis=0, concat_axis=0, tiled=True)
    combined = jnp.dot(
        slot_table,
        returned.reshape(expert_count * capacity, -1),
        preferred_element_type=jnp.float32,
    )
    stream_after = stream + gate_values[:, None] * combined
    return (
        (normed_low, logits, chosen, gate_values, slot_table, combined, hidden_pre, received),
        stream_after,
    )


def sparse_backward(grad_stream, stream, gain_row, router_full, in_full, out_experts, kept_state):
    normed_low, logits, chosen, gate_values, slot_table, combined, hidden_pre, received = kept_state
    grad_gates = jnp.sum(grad_stream * combined, axis=-1)
    grad_combined = (gate_values[:, None] * grad_stream).astype(jnp.bfloat16)
    outgoing = jnp.einsum(
        "ts,td->sd", slot_table, grad_combined, preferred_element_type=jnp.float32
    ).astype(jnp.bfloat16)
    grad_produced = lax.all_to_all(
        outgoing.reshape(received.shape), "expert", split_axis=0, concat_axis=0, tiled=True
    )
    gelu_value, gelu_pull = jax.vjp(gelu_tanh, hidden_pre)
    hidden_low = gelu_value.astype(jnp.bfloat16)
    grad_w_out = jnp.einsum(
        "secf,secd->efd", hidden_low, grad_produced, preferred_element_type=jnp.float32
    )
    grad_hidden = (
        jnp.einsum("secd,efd->secf", grad_produced, out_experts, preferred_element_type=jnp.float32)
        .astype(jnp.bfloat16)
        .astype(jnp.float32)
    )
    grad_pre = gelu_pull(grad_hidden)[0].astype(jnp.bfloat16)
    grad_w_in = jnp.einsum("secd,secf->edf", received, grad_pre, preferred_element_type=jnp.float32)
    grad_received = jnp.einsum(
        "secf,edf->secd", grad_pre, in_full, preferred_element_type=jnp.float32
    ).astype(jnp.bfloat16)
    grad_sent = lax.all_to_all(grad_received, "expert", split_axis=0, concat_axis=0, tiled=True)
    grad_normed = jnp.dot(
        slot_table, grad_sent.reshape(slot_table.shape[1], -1), preferred_element_type=jnp.float32
    )
    gate_again, gate_pull = jax.vjp(gate_of, logits, chosen)
    grad_logits = gate_pull(grad_gates)[0].astype(jnp.bfloat16)
    grad_router = jnp.einsum(
        "td,te->de", normed_low, grad_logits, preferred_element_type=jnp.float32
    )
    grad_normed = grad_normed + jnp.einsum(
        "te,de->td", grad_logits, router_full, preferred_element_type=jnp.float32
    )
    grad_input, grad_gain = norm_backward(grad_normed, stream, gain_row)
    return (grad_stream + grad_input, grad_gain, grad_router, grad_w_in, grad_w_out)


def on_device(
    tokens_in,
    segment_ids,
    expert_index,
    expert_slot,
    attn_gain,
    qkv_weight,
    out_weight,
    rel_bias,
    ffn_gain,
    ffn_in,
    ffn_out,
    router,
    expert_in,
    expert_out,
    cotangent,
):
    dense_full = (
        lax.all_gather(attn_gain, ("expert", "dp"), axis=1, tiled=True),
        lax.all_gather(qkv_weight, ("expert", "dp"), axis=0, tiled=True),
        lax.all_gather(out_weight, ("expert", "dp"), axis=0, tiled=True),
        lax.all_gather(ffn_gain, ("expert", "dp"), axis=1, tiled=True),
        lax.all_gather(ffn_in, ("expert", "dp"), axis=0, tiled=True),
        lax.all_gather(ffn_out, ("expert", "dp"), axis=0, tiled=True),
        lax.all_gather(router, ("expert", "dp"), axis=0, tiled=True),
    )
    expert_full = (
        lax.all_gather(expert_in, "dp", axis=1, tiled=True),
        lax.all_gather(expert_out, "dp", axis=1, tiled=True),
    )
    pair_table = pair_onehot()
    bias_full = jnp.einsum("ijb,bh->hij", pair_table, rel_bias, precision=PRECISE)
    expert_count = lax.axis_size("expert") * expert_in.shape[0]
    stream_zero = tokens_in.astype(jnp.float32)
    attn_zero = attention_forward(
        stream_zero,
        dense_full[0][0],
        dense_full[1][:, 0],
        dense_full[2][:, 0],
        segment_ids,
        bias_full,
    )
    dense_zero = dense_forward(attn_zero[4], dense_full[3][0], dense_full[4], dense_full[5])
    attn_one = attention_forward(
        dense_zero[2],
        dense_full[0][1],
        dense_full[1][:, 1],
        dense_full[2][:, 1],
        segment_ids,
        bias_full,
    )
    sparse_one, stream_two = sparse_forward(
        attn_one[4],
        dense_full[3][1],
        dense_full[6],
        expert_full[0],
        expert_full[1],
        expert_index,
        expert_slot,
        expert_count,
    )
    dense_full = (
        lax.all_gather(attn_gain, ("expert", "dp"), axis=1, tiled=True),
        lax.all_gather(qkv_weight, ("expert", "dp"), axis=0, tiled=True),
        lax.all_gather(out_weight, ("expert", "dp"), axis=0, tiled=True),
        lax.all_gather(ffn_gain, ("expert", "dp"), axis=1, tiled=True),
        lax.all_gather(ffn_in, ("expert", "dp"), axis=0, tiled=True),
        lax.all_gather(ffn_out, ("expert", "dp"), axis=0, tiled=True),
        lax.all_gather(router, ("expert", "dp"), axis=0, tiled=True),
    )
    expert_full = (
        lax.all_gather(expert_in, "dp", axis=1, tiled=True),
        lax.all_gather(expert_out, "dp", axis=1, tiled=True),
    )
    grad_top = cotangent.astype(jnp.float32)
    grad_middle, ffn_gain_one, router_term, expert_in_term, expert_out_term = sparse_backward(
        grad_top,
        attn_one[4],
        dense_full[3][1],
        dense_full[6],
        expert_full[0],
        expert_full[1],
        sparse_one,
    )
    expert_sums = (
        lax.psum_scatter(
            expert_in_term.astype(jnp.bfloat16), "dp", scatter_dimension=1, tiled=True
        ).astype(jnp.float32),
        lax.psum_scatter(
            expert_out_term.astype(jnp.bfloat16), "dp", scatter_dimension=1, tiled=True
        ).astype(jnp.float32),
    )
    grad_one, attn_gain_one, qkv_one, out_one, pairs_one = attention_backward(
        grad_middle,
        dense_zero[2],
        dense_full[0][1],
        dense_full[1][:, 1],
        dense_full[2][:, 1],
        segment_ids,
        bias_full,
        attn_one,
    )
    grad_half, ffn_gain_zero, ffn_in_term, ffn_out_term = dense_backward(
        grad_one, attn_zero[4], dense_full[3][0], dense_full[4], dense_full[5], dense_zero
    )
    grad_zero, attn_gain_zero, qkv_zero, out_zero, pairs_zero = attention_backward(
        grad_half,
        stream_zero,
        dense_full[0][0],
        dense_full[1][:, 0],
        dense_full[2][:, 0],
        segment_ids,
        bias_full,
        attn_zero,
    )
    gain_terms = jnp.stack([attn_gain_zero, attn_gain_one])
    qkv_terms = jnp.stack([qkv_zero, qkv_one], axis=1)
    out_terms = jnp.stack([out_zero, out_one], axis=1)
    ffn_gain_terms = jnp.stack([ffn_gain_zero, ffn_gain_one])
    dense_sums = (
        lax.psum_scatter(gain_terms, ("expert", "dp"), scatter_dimension=1, tiled=True),
        lax.psum_scatter(qkv_terms, ("expert", "dp"), scatter_dimension=0, tiled=True),
        lax.psum_scatter(out_terms, ("expert", "dp"), scatter_dimension=0, tiled=True),
        lax.psum_scatter(ffn_gain_terms, ("expert", "dp"), scatter_dimension=1, tiled=True),
        lax.psum_scatter(ffn_in_term, ("expert", "dp"), scatter_dimension=0, tiled=True),
        lax.psum_scatter(ffn_out_term, ("expert", "dp"), scatter_dimension=0, tiled=True),
        lax.psum_scatter(router_term, ("expert", "dp"), scatter_dimension=0, tiled=True),
    )
    attn_gain_sum = dense_sums[0]
    qkv_sum = dense_sums[1]
    out_sum = dense_sums[2]
    ffn_gain_sum = dense_sums[3]
    ffn_in_sum = dense_sums[4]
    ffn_out_sum = dense_sums[5]
    router_sum = dense_sums[6]
    bias_term = jnp.einsum("hij,ijb->bh", pairs_zero + pairs_one, pair_table, precision=PRECISE)
    bias_sum = lax.psum(bias_term, ("expert", "dp"))
    return (
        stream_two.astype(jnp.bfloat16),
        grad_zero,
        attn_gain_sum,
        qkv_sum,
        out_sum,
        bias_sum,
        ffn_gain_sum,
        ffn_in_sum,
        ffn_out_sum,
        router_sum,
        expert_sums[0],
        expert_sums[1],
    )


def solution(mesh):
    placed = (
        P(("expert", "dp"), None),
        P(("expert", "dp"), None),
        P(("expert", "dp")),
        P(("expert", "dp")),
        P(None, ("expert", "dp")),
        P(("expert", "dp"), None, None),
        P(("expert", "dp"), None, None),
        P(),
        P(None, ("expert", "dp")),
        P(("expert", "dp"), None),
        P(("expert", "dp"), None),
        P(("expert", "dp"), None),
        P("expert", "dp", None),
        P("expert", "dp", None),
        P(("expert", "dp"), None),
    )
    return jax.shard_map(
        on_device,
        mesh=mesh,
        in_specs=placed,
        out_specs=(
            P(("expert", "dp"), None),
            P(("expert", "dp"), None),
            P(None, ("expert", "dp")),
            P(("expert", "dp"), None, None),
            P(("expert", "dp"), None, None),
            P(),
            P(None, ("expert", "dp")),
            P(("expert", "dp"), None),
            P(("expert", "dp"), None),
            P(("expert", "dp"), None),
            P("expert", "dp", None),
            P("expert", "dp", None),
        ),
        check_vma=False,
    )
```

profile of v0, /device:TPU:0, one launch (start us, length us, event | category | flops | bytes accessed | tf_op | source)
XLA Modules:
  0.0 1217.4 jit_solution(8752431234132477929)
XLA Ops:
  15.7 43.3 %all-gather = bf16[32,24,2]{1,2,0:T(2,128)(2,1)S(1)} all-gather(bf16[1,24,2]{1,2,0:T(2,128)(2,1)} %bitcast.305), channel_id=1, replica_groups=mesh['expert'=4,'dp'=8] {'expert','dp'}, dimensions={0}, use_global_device_ids=true | all-gather | bytes 3168 | tf_op jit(solution)/shard_map/all_gather | solution.py:322
  59.1 36.8 %all-gather.1 = bf16[32,24,2]{1,2,0:T(2,128)(2,1)S(1)} all-gather(bf16[1,24,2]{1,2,0:T(2,128)(2,1)} %bitcast.306), channel_id=1, replica_groups=mesh['expert'=4,'dp'=8] {'expert','dp'}, dimensions={0}, use_global_device_ids=true | all-gather | bytes 3168 | tf_op jit(solution)/shard_map/all_gather | solution.py:325
  97.0 13.8 %fusion.3 = f32[512,512,12]{1,2,0:T(8,128)} fusion(s32[512,512]{1,0:T(8,128)S(1)} %fusion.125, f32[32,12]{0,1:T(8,128)S(1)} %copy-done), kind=kOutput, calls=%fused_computation.4 | convolution fusion | flops 1216348160 | bytes 13633024 | tf_op jit(solution)/shard_map/ijb,bh->hij/dot_general | solution.py:335
  110.9 17.9 %copy.89 = f32[512,512,12]{0,1,2:T(8,128)} copy(f32[512,512,12]{1,2,0:T(8,128)} %fusion.3) | data formatting | bytes 25165824 | tf_op jit(solution)/shard_map/ijb,bh->hij/dot_general | solution.py:335
  150.4 62.3 %all-gather.14.cloned.1.call-done = bf16[768,3072]{1,0:T(8,128)(2,1)} async-done(((bf16[24,3072]{1,0:T(8,128)(2,1)}), bf16[768,3072]{1,0:T(8,128)(2,1)}) %all-gather.14.cloned.1.call-update) | async-done | bytes 4718608 | tf_op jit(solution)/shard_map/all_gather | solution.py:326
  219.7 58.4 %all-gather.16.cloned.1.call-done = bf16[3072,768]{1,0:T(8,128)(2,1)} async-done(((bf16[96,768]{1,0:T(8,128)(2,1)}), bf16[3072,768]{1,0:T(8,128)(2,1)}) %all-gather.16.cloned.1.call-update) | async-done | bytes 4718608 | tf_op jit(solution)/shard_map/all_gather | solution.py:327
  312.2 18.0 %all-gather.18.cloned.1.call-done = bf16[1,768,3072]{2,1,0:T(8,128)(2,1)} async-done(((bf16[1,96,3072]{2,1,0:T(8,128)(2,1)}), bf16[1,768,3072]{2,1,0:T(8,128)(2,1)}) %all-gather.18.cloned.1.call-update) | async-done | bytes 4718608 | tf_op jit(solution)/shard_map/all_gather | solution.py:331
  337.4 44.9 %all-gather.20.cloned.1.call-done = bf16[1,3072,768]{2,1,0:T(8,128)(2,1)} async-done(((bf16[1,384,768]{2,1,0:T(8,128)(2,1)}), bf16[1,3072,768]{2,1,0:T(8,128)(2,1)}) %all-gather.20.cloned.1.call-update) | async-done | bytes 4718608 | tf_op jit(solution)/shard_map/all_gather | solution.py:332
  382.2 8.8 fusion.114
  395.3 39.6 %all-gather.2 = bf16[32,24,4]{1,2,0:T(4,128)(2,1)S(1)} all-gather(bf16[1,24,4]{1,2,0:T(4,128)(2,1)S(1)} %bitcast.304), channel_id=1, replica_groups=mesh['expert'=4,'dp'=8] {'expert','dp'}, dimensions={0}, use_global_device_ids=true | all-gather | bytes 6336 | tf_op jit(solution)/shard_map/all_gather | solution.py:328
  439.3 14.9 %all_to_all.20 = bf16[4,1,128,768]{3,2,1,0:T(8,128)(2,1)S(1)} all-to-all(bf16[4,1,128,768]{3,2,1,0:T(8,128)(2,1)S(1)} %bitcast.300), channel_id=1, replica_groups=mesh['expert'=4,'dp'=8] {'expert'}, dimensions={0} | all-to-all | bytes 1572864 | tf_op jit(solution)/shard_map/all_to_all | solution.py:270
  470.9 10.1 all-to-all-done.3
  494.4 16.7 %subtract_multiply_fusion.1 = f32[12,512,512]{1,2,0:T(8,128)} fusion(f32[12,512,512]{1,2,0:T(8,128)} %copy-done.3, f32[12,512]{1,0:T(8,128)S(1)} %log_add_fusion.1, bf16[512,12,64]{0,2,1:T(8,128)(2,1)S(1)} %bitcast.263, bf16[512,12,64]{0,2,1:T(8,128)(2,1)} %bitcast.275), kind=kOutput, calls=%fused_computation.18 | convolution fusion | flops 821041664 | bytes 26763264 | tf_op jit(solution)/shard_map/while/body/eval_jaxpr/sub | solution.py:113
  526.0 8.7 fusion.20
  565.2 26.5 %fusion.200 = (f32[12,512,512]{1,2,0:T(8,128)}, f32[12,512,512]{1,2,0:T(8,128)}) fusion(f32[12,512,512]{1,2,0:T(8,128)} %subtract_multiply_fusion.1, f32[12,512,512]{1,2,0:T(8,128)} %copy-done.2, f32[12,512]{1,0:T(8,128)S(1)} %log_add_fusion, bf16[512,12,64]{0,2,1:T(8,128)(2,1)S(1)} %bitcast.260, bf16[512,12,64]{0,2,1:T(8,128)(2,1)} %bitcast.265), kind=kOutput, calls=%fused_computation.263 | convolution fusion | flops 824187392 | bytes 51929088 | tf_op jit(solution)/shard_map/while/body/eval_jaxpr/sub | solution.py:113
  618.6 11.1 pad_maximum_fusion
  629.7 10.1 fusion.151
  654.7 18.5 %copy.110 = f32[12,512,512]{2,0,1:T(8,128)} copy(f32[12,512,512]{1,2,0:T(8,128)} %get-tuple-element.212) | data formatting | bytes 25165824 | tf_op jit(solution)/shard_map/add | solution.py:439
  673.3 20.2 %fusion.124 = f32[32,12]{0,1:T(8,128)S(1)} fusion(f32[12,512,512]{2,0,1:T(8,128)} %copy.110, s32[512,512]{1,0:T(8,128)S(1)} %copy-done.11), kind=kOutput, calls=%fused_computation.165 | convolution fusion | flops 1216348160 | bytes 13633024 | tf_op jit(solution)/shard_map/hij,ijb->bh/dot_general | solution.py:439
  693.5 38.9 %all-reduce.3 = (f32[2,768]{1,0:T(2,128)S(1)}, f32[32,12]{0,1:T(8,128)}, f32[2,768]{1,0:T(2,128)S(1)}, f32[768,4]{0,1:T(4,128)S(1)}) all-reduce(f32[2,768]{1,0:T(2,128)S(1)} %pad_maximum_fusion.8, f32[32,12]{0,1:T(8,128)S(1)} %fusion.124, ...), channel_id=2, replica_groups=mesh['expert'=4,'dp'=8] {'expert','dp'}, use_global_device_ids=true, to_apply=%region_21.22.clone | all-reduce | flops 6528 | bytes 52224
  740.6 19.1 %reduce-scatter.18.cloned.1.call-done = bf16[1,96,3072]{2,1,0:T(8,128)(2,1)} async-done(((bf16[1,768,3072]{2,1,0:T(8,128)(2,1)}), bf16[1,96,3072]{2,1,0:T(8,128)(2,1)}) %reduce-scatter.18.cloned.1.call-update) | async-done | bytes 589840 | tf_op jit(solution)/shard_map/reduce_scatter | solution.py:389
  761.9 165.8 %reduce-scatter.10.cloned.1.call-done = f32[24,2,2304]{2,0,1:T(8,128)} async-done(((f32[768,2,2304]{2,0,1:T(8,128)}), f32[24,2,2304]{2,0,1:T(8,128)}) %reduce-scatter.10.cloned.1.call-update) | async-done | bytes 442384 | tf_op jit(solution)/shard_map/reduce_scatter | solution.py:425
  929.7 139.7 %reduce-scatter.16.cloned.1.call-done = f32[96,768]{1,0:T(8,128)} async-done(((f32[3072,768]{1,0:T(8,128)}), f32[96,768]{1,0:T(8,128)}) %reduce-scatter.16.cloned.1.call-update) | async-done | bytes 294928 | tf_op jit(solution)/shard_map/reduce_scatter | solution.py:429
  1069.4 141.0 %reduce-scatter.14.cloned.1.call-done = f32[24,3072]{1,0:T(8,128)} async-done(((f32[768,3072]{1,0:T(8,128)}), f32[24,3072]{1,0:T(8,128)}) %reduce-scatter.14.cloned.1.call-update) | async-done | bytes 294928 | tf_op jit(solution)/shard_map/reduce_scatter | solution.py:428
  (296 shorter events, 216.7 us)
Async XLA Ops:
  7.2 89.9 %copy-start = (f32[32,12]{0,1:T(8,128)S(1)}, f32[32,12]{0,1:T(8,128)}, u32[]{:S(2)}) copy-start(f32[32,12]{0,1:T(8,128)} %param.22) | copy-start | bytes 4612
  7.2 121.6 %all-gather.10.cloned.1.call-start = ((), (), s32[]{:S(2)}) async-start(), calls=%async_computation.10 | async-start | bytes 7299072 | tf_op jit(solution)/shard_map/all_gather | solution.py:323
  8.9 139.0 %all-gather.12.cloned.1.call-start = ((), (), s32[]{:S(2)}) async-start(), calls=%async_computation.11 | async-start | bytes 2433024 | tf_op jit(solution)/shard_map/all_gather | solution.py:324
  10.5 202.2 %all-gather.14.cloned.1.call-start = ((), (), s32[]{:S(2)}) async-start(), calls=%async_computation.12 | async-start | bytes 4866048 | tf_op jit(solution)/shard_map/all_gather | solution.py:326
  11.2 266.9 %all-gather.16.cloned.1.call-start = ((), (), s32[]{:S(2)}) async-start(), calls=%async_computation.13 | async-start | bytes 4866048 | tf_op jit(solution)/shard_map/all_gather | solution.py:327
  11.8 318.3 %all-gather.18.cloned.1.call-start = ((), (), s32[]{:S(2)}) async-start(), calls=%async_computation.14 | async-start | bytes 5308416 | tf_op jit(solution)/shard_map/all_gather | solution.py:331
  12.4 369.8 %all-gather.20.cloned.1.call-start = ((), (), s32[]{:S(2)}) async-start(), calls=%async_computation.15 | async-start | bytes 5308416 | tf_op jit(solution)/shard_map/all_gather | solution.py:332
  13.9 97.0 %copy-start.10 = (s32[512,512]{1,0:T(8,128)}, s32[512,512]{1,0:T(8,128)S(1)}, u32[]{:S(2)}) copy-start(s32[512,512]{1,0:T(8,128)S(1)} %fusion.125) | copy-start | bytes 3145732
  15.7 113.2 %copy-start.61 = (f32[512]{0:T(512)}, f32[512]{0:T(512)S(1)}, u32[]{:S(2)}) copy-start(f32[512]{0:T(512)S(1)} %fusion.169) | copy-start | bytes 6148
  59.1 69.8 %copy-start.59 = (f32[768]{0:T(1024)}, f32[768]{0:T(1024)S(1)}, u32[]{:S(2)}) copy-start(f32[768]{0:T(1024)S(1)} %get-tuple-element.181) | copy-start | bytes 9220
  147.9 71.8 %copy-start.39 = (bf16[12,64,512]{2,1,0:T(8,128)(2,1)}, bf16[12,64,512]{2,1,0:T(8,128)(2,1)S(1)}, u32[]{:S(2)}) copy-start(bf16[12,64,512]{2,1,0:T(8,128)(2,1)S(1)} %fusion.109) | copy-start | bytes 2359300
  150.4 69.3 %copy-start.63 = (f32[512]{0:T(512)}, f32[512]{0:T(512)S(1)}, u32[]{:S(2)}) copy-start(f32[512]{0:T(512)S(1)} %get-tuple-element.196) | copy-start | bytes 6148
  150.4 127.7 %copy-start.6 = (f32[512,768]{1,0:T(8,128)}, f32[512,768]{1,0:T(8,128)S(1)}, u32[]{:S(2)}) copy-start(f32[512,768]{1,0:T(8,128)S(1)} %get-tuple-element.197) | copy-start | bytes 4718596
  307.1 127.9 %copy-start.20 = (bf16[512,768]{1,0:T(8,128)(2,1)}, bf16[512,768]{1,0:T(8,128)(2,1)S(1)}, u32[]{:S(2)}) copy-start(bf16[512,768]{1,0:T(8,128)(2,1)S(1)} %multiply_convert_fusion.7) | copy-start | bytes 2359300
  308.7 21.5 %all-to-all-start = ((bf16[4,1,128,768]{3,2,1,0:T(8,128)(2,1)}), bf16[4,1,128,768]{3,2,1,0:T(8,128)(2,1)S(1)}, u32[]{:S(2)}, u32[]{:S(2)}) async-start(bf16[4,1,128,768]{3,2,1,0:T(8,128)(2,1)} %bitcast.299), calls=%async_computation | async-start | bytes 1572864 | tf_op jit(solution)/shard_map/all_to_all | solution.py:246
  391.1 44.3 %all-to-all-start.1 = ((bf16[4,1,128,768]{3,2,1,0:T(8,128)(2,1)}), bf16[4,1,128,768]{3,2,1,0:T(8,128)(2,1)}, u32[]{:S(2)}, u32[]{:S(2)}) async-start(bf16[4,1,128,768]{3,2,1,0:T(8,128)(2,1)} %fusion.114), calls=%async_computation.1 | async-start | bytes 1572864 | tf_op jit(solution)/shard_map/all_to_all | solution.py:250
  467.4 13.7 %all-to-all-start.3 = ((bf16[4,1,128,768]{3,2,1,0:T(8,128)(2,1)}), bf16[4,1,128,768]{3,2,1,0:T(8,128)(2,1)S(1)}, u32[]{:S(2)}, u32[]{:S(2)}) async-start(bf16[4,1,128,768]{3,2,1,0:T(8,128)(2,1)} %fusion.119), calls=%async_computation.3 | async-start | bytes 1572864 | tf_op jit(solution)/shard_map/all_to_all | solution.py:288
  470.9 265.9 %reduce-scatter.12.cloned.1.call-start = ((), (), s32[]{:S(2)}) async-start(), calls=%async_computation.17 | async-start | bytes 4866048 | tf_op jit(solution)/shard_map/reduce_scatter | solution.py:426
  542.4 196.0 %reduce-scatter.20.cloned.1.call-start = ((), (), s32[]{:S(2)}) async-start(), calls=%async_computation.21 | async-start | bytes 5308416 | tf_op jit(solution)/shard_map/reduce_scatter | solution.py:392
  551.9 207.8 %reduce-scatter.18.cloned.1.call-start = ((), (), s32[]{:S(2)}) async-start(), calls=%async_computation.20 | async-start | bytes 5308416 | tf_op jit(solution)/shard_map/reduce_scatter | solution.py:389
  559.3 368.4 %reduce-scatter.10.cloned.1.call-start = ((), (), s32[]{:S(2)}) async-start(), calls=%async_computation.16 | async-start | bytes 14598144 | tf_op jit(solution)/shard_map/reduce_scatter | solution.py:425
  629.7 439.7 %reduce-scatter.16.cloned.1.call-start = ((), (), s32[]{:S(2)}) async-start(), calls=%async_computation.19 | async-start | bytes 9732096 | tf_op jit(solution)/shard_map/reduce_scatter | solution.py:429
  639.9 570.5 %reduce-scatter.14.cloned.1.call-start = ((), (), s32[]{:S(2)}) async-start(), calls=%async_computation.18 | async-start | bytes 9732096 | tf_op jit(solution)/shard_map/reduce_scatter | solution.py:428
  733.7 476.7 %copy-start.1 = (f32[32,12]{0,1:T(8,128)S(1)}, f32[32,12]{0,1:T(8,128)}, u32[]{:S(2)}) copy-start(f32[32,12]{0,1:T(8,128)} %param.22) | copy-start | bytes 4612
  (72 other events, 703.0 us)
Sparse Core Ops, SparseCore 0:
  11.8 75.4 all-gather.9
  91.1 56.0 all-gather.11
  150.1 62.5 all-gather.13
  215.6 62.4 all-gather.15
  279.6 50.5 all-gather.17
  331.7 50.5 all-gather.19
  542.6 104.2 reduce-scatter.11
  649.2 54.0 reduce-scatter.19
  705.8 53.8 reduce-scatter.17
  766.6 161.0 reduce-scatter.9
  935.2 134.1 reduce-scatter.15
  1075.7 134.6 reduce-scatter.13
where the time goes:
time: 1220 us
  waiting for transfers between devices  662 us (54%)
  matrix products  256 us (21%)
  blocking collectives  173 us (14%)
  local copies, waits for them, and re-layouts  65.8 us (5%)
  other arithmetic  32.8 us (3%)
  between operations  15.6 us (1%)
    reduce_scatter x1, waiting for transfers between devices, on_device(): lax.psum_scatter(qkv_terms, ('expert', 'dp'), scatter_dimension=0, tiled=...  166 us
    reduce_scatter x1, waiting for transfers between devices, on_device(): lax.psum_scatter(ffn_in_term, ('expert', 'dp'), scatter_dimension=0, tile...  141 us
    reduce_scatter x1, waiting for transfers between devices, on_device(): lax.psum_scatter(ffn_out_term, ('expert', 'dp'), scatter_dimension=0, til...  140 us
    all_gather x1, waiting for transfers between devices, on_device(): lax.all_gather(ffn_in, ('expert', 'dp'), axis=0, tiled=True)  62.3 us
    all_gather x1, waiting for transfers between devices, on_device(): lax.all_gather(ffn_out, ('expert', 'dp'), axis=0, tiled=True)  58.4 us
    all_gather x1, waiting for transfers between devices, on_device(): lax.all_gather(expert_out, 'dp', axis=1, tiled=True)  44.9 us
    all_gather x1, blocking collectives, on_device(): lax.all_gather(attn_gain, ('expert', 'dp'), axis=1, tiled=True)  43.3 us
    sub x2, matrix products, one_block(): grad_weights - jnp.sum(weights_now * grad_weights, axis=-1, keepdims=True)  43.1 us
  transfers between devices with their start and end apart: 15, of which 9 were waited for; matrix products, arithmetic and copies ran while one was open for 21% of the time, Pallas kernels for 0%

commit v1 on v0

v1 whole, which is shorter than its diff:
```python
import functools
import math

import jax
import jax.numpy as jnp
from jax import lax
from jax.experimental import pallas as pl
from jax.experimental.pallas import tpu as pltpu
from jax.sharding import Mesh, PartitionSpec as P

HEADS = 12
DH = 64
BUCKETS = 32
SEQ = 512


EPSILON = 1e-06
NEG_FILL = -1e30
PRECISE = lax.Precision.HIGHEST


def bucket_of(offset):
    distance = jnp.abs(offset)
    far_bucket = jnp.full_like(distance, 8)
    for level_id in range(1, 8):
        far_bucket = far_bucket + (distance * distance >= 64 * 2**level_id).astype(jnp.int32)
    near_bucket = jnp.where(distance < 8, distance, far_bucket)
    return near_bucket + 16 * (offset > 0).astype(jnp.int32)


def norm_scale(stream, gain_row):
    inverse = lax.rsqrt(jnp.mean(stream * stream, axis=-1, keepdims=True) + EPSILON)
    return stream * inverse * gain_row


def norm_backward(grad_normed, stream, gain_row):
    normed_again, norm_pull = jax.vjp(norm_scale, stream, gain_row.astype(jnp.float32))
    grad_input, grad_gain = norm_pull(grad_normed)
    return (grad_input, grad_gain)


def gelu_tanh(value):
    return jax.nn.gelu(value, approximate=True)


def gate_of(logits, chosen):
    return jnp.sum(jax.nn.softmax(logits, axis=-1) * chosen, axis=-1)


EXPERT_AXES = ("ey", "ex")
DATA_AXES = ("z", "core")
ALL_AXES = ("ey", "ex", "z", "core")
SPAN = 2 * SEQ
ROWS = 128
VMEM_BYTES = 48 * 1024 * 1024
BF16 = jnp.bfloat16
F32 = jnp.float32
ATTEND_COST = 22 * 10**9


def swap_with(value, axes, count, flip):
    return lax.ppermute(value, axes, [(i, i ^ flip) for i in range(count)])


def place_kernel(count, axis, cuts, me_ref, *refs):
    sources = refs[:count]
    targets = refs[count : count + len(cuts)]
    held, in_sems, out_sems = refs[count + len(cuts) :]
    arriving = [
        pltpu.make_async_copy(sources[flip], held.at[flip], in_sems.at[flip]) for flip in range(count)
    ]
    for copy in arriving:
        copy.start()
    leaving = []
    for flip in range(count):
        slot = me_ref[0] ^ flip
        arriving[flip].wait()
        for cut_id, group in enumerate(cuts):
            target = targets[cut_id]
            target = target.at[slot] if axis == 0 else target.at[:, slot]
            for part_id, (first, last) in enumerate(group):
                origin = held.at[flip]
                if axis == 1:
                    origin = origin.at[:, :, first:last]
                spot = target if len(group) == 1 else target.at[:, part_id]
                copy = pltpu.make_async_copy(origin, spot, out_sems.at[flip, cut_id, part_id])
                copy.start()
                leaving.append(copy)
    for copy in leaving:
        copy.wait()


def place(parts, me, axis=0, cuts=None):
    shape = parts[0].shape
    groups = cuts or (((0, shape[-1]),),)
    outs = []
    for group in groups:
        own = shape[:-1] + (group[0][1] - group[0][0],)
        lead = own[:axis] + (len(parts),) + ((len(group),) if len(group) > 1 else ())
        outs.append(jax.ShapeDtypeStruct(lead + own[axis:], parts[0].dtype))
    moved = sum(math.prod(o.shape) for o in outs) * 4
    most = max(len(group) for group in groups)
    placed = pl.pallas_call(
        functools.partial(place_kernel, len(parts), axis, groups),
        out_shape=outs,
        in_specs=[pl.BlockSpec(memory_space=pltpu.SMEM)]
        + [pl.BlockSpec(memory_space=pl.ANY)] * len(parts),
        out_specs=[pl.BlockSpec(memory_space=pl.ANY)] * len(outs),
        scratch_shapes=[
            pltpu.VMEM((len(parts),) + shape, parts[0].dtype),
            pltpu.SemaphoreType.DMA((len(parts),)),
            pltpu.SemaphoreType.DMA((len(parts), len(groups), most)),
        ],
        compiler_params=pltpu.CompilerParams(vmem_limit_bytes=VMEM_BYTES),
        cost_estimate=pl.CostEstimate(flops=0, bytes_accessed=2 * moved, transcendentals=0),
    )(me.astype(jnp.int32).reshape(1), *parts)
    return placed if cuts else placed[0]


def together(*values):
    return lax.optimization_barrier(values)


def gather_z(shard):
    depth = lax.axis_size("z")
    along = [shard] + [swap_with(shard, "z", depth, k) for k in range(1, depth)]
    return place(along, lax.axis_index("z"))


def gather_across(line):
    experts = lax.axis_size(EXPERT_AXES)
    across = [line] + [swap_with(line, EXPERT_AXES, experts, k) for k in range(1, experts)]
    half = place(across, lax.axis_index(EXPERT_AXES))
    return half.reshape((-1,) + line.shape[1:])


def gather_core(half, cuts):
    other = swap_with(half, "core", 2, 1)
    whole = place([half, other], lax.axis_index("core"), axis=1, cuts=cuts)
    return [part.reshape(-1, part.shape[-1]) for part in whole]


def tree_sum(terms):
    while len(terms) > 1:
        terms = [terms[i] + terms[i + 1] for i in range(0, len(terms), 2)]
    return terms[0]


def scatter_stage(pieces, axes, axis):
    count = lax.axis_size(axes)
    me = lax.axis_index(axes)

    def of(slot):
        own = [lax.dynamic_index_in_dim(p, slot, axis, keepdims=False) for p in pieces]
        return own[0] if len(own) == 1 else jnp.concatenate(own, axis=-1)

    terms = [of(me)]
    for flip in range(1, count):
        terms.append(swap_with(of(me ^ flip), axes, count, flip))
    return tree_sum([t.astype(F32) for t in terms])


def scatter_core(grads):
    groups = lax.axis_size(EXPERT_AXES) * lax.axis_size("z")
    pieces = []
    for grad, blocks in grads:
        rows = grad.shape[0] // (2 * groups * blocks)
        split = grad.reshape(groups, 2, blocks, rows, grad.shape[-1])
        pieces.extend(split[:, :, block] for block in range(blocks))
    return scatter_stage(pieces, "core", 1).astype(BF16)


def scatter_across(half):
    experts = lax.axis_size(EXPERT_AXES)
    return scatter_stage([half.reshape((experts, -1) + half.shape[1:])], EXPERT_AXES, 0).astype(BF16)


def scatter_z(line):
    return scatter_stage([line], "z", 0)


def sum_everywhere(value):
    for axes in ("core", EXPERT_AXES, "z"):
        count = lax.axis_size(axes)
        value = tree_sum([value] + [swap_with(value, axes, count, k) for k in range(1, count)])
    return value


def bias_kernel(row_ref, seg_col_ref, seg_row_ref, out_ref):
    offsets = jnp.broadcast_to(row_ref[0], (ROWS, SPAN))
    seg_row = seg_row_ref[...]
    for first in range(0, SEQ, ROWS):
        turned = pltpu.roll(offsets, first, 1, stride=1, stride_axis=0)[:, :SEQ]
        same = seg_col_ref[first : first + ROWS, :] == seg_row
        out_ref[0, first : first + ROWS, :] = jnp.where(same, turned, NEG_FILL)


def offset_onehot():
    columns = jnp.arange(SPAN, dtype=jnp.int32)
    offsets = jnp.where(columns < SEQ, columns, columns - SPAN)
    return (bucket_of(offsets)[:, None] == jnp.arange(BUCKETS, dtype=jnp.int32)[None, :]).astype(F32)


def masked_bias(rel_bias, segments):
    by_offset = jnp.dot(offset_onehot(), rel_bias, precision=PRECISE).T
    return pl.pallas_call(
        bias_kernel,
        grid=(HEADS,),
        in_specs=[
            pl.BlockSpec((1, 1, SPAN), lambda h: (h, 0, 0)),
            pl.BlockSpec((SEQ, 1), lambda h: (0, 0)),
            pl.BlockSpec((1, SEQ), lambda h: (0, 0)),
        ],
        out_specs=pl.BlockSpec((1, SEQ, SEQ), lambda h: (h, 0, 0)),
        out_shape=jax.ShapeDtypeStruct((HEADS, SEQ, SEQ), F32),
        compiler_params=pltpu.CompilerParams(vmem_limit_bytes=VMEM_BYTES),
        cost_estimate=pl.CostEstimate(flops=ATTEND_COST // 3, bytes_accessed=HEADS * SEQ * SEQ * 8, transcendentals=0),
    )(by_offset.reshape(HEADS, 1, SPAN), segments.reshape(SEQ, 1), segments.reshape(1, SEQ))


def dot_nt(a, b):
    return lax.dot_general(a, b, (((1,), (1,)), ((), ())), preferred_element_type=F32)


def dot_tn(a, b):
    return lax.dot_general(a, b, (((0,), (0,)), ((), ())), preferred_element_type=F32)


def half_masks(rows):
    lanes = lax.broadcasted_iota(jnp.int32, (rows, 2 * DH), 1)
    return (lanes < DH, lanes >= DH)


def attend_kernel(q_ref, k_ref, v_ref, bias_ref, mixed_ref, prob_ref):
    keys = k_ref[...]
    values = v_ref[...]
    masks = half_masks(ROWS)
    for first in range(0, SEQ, ROWS):
        rows = slice(first, first + ROWS)
        query = q_ref[rows, :] * BF16(DH ** (-0.5))
        mixed = []
        for head in range(2):
            own = jnp.where(masks[head], query, jnp.zeros_like(query))
            scores = dot_nt(own, keys) + bias_ref[head, rows, :]
            grown = jnp.exp(scores - jnp.max(scores, axis=-1, keepdims=True))
            prob = (grown * (1.0 / jnp.sum(grown, axis=-1, keepdims=True))).astype(BF16)
            prob_ref[head, rows, :] = prob
            mixed.append(jnp.dot(prob, values, preferred_element_type=F32))
        mixed_ref[rows, :] = jnp.where(masks[0], mixed[0], mixed[1]).astype(BF16)


PAIRS = HEADS // 2


def attend_forward(packed, bias):
    def columns(base):
        return pl.BlockSpec((SEQ, 2 * DH), lambda p: (0, base + p))

    return pl.pallas_call(
        attend_kernel,
        grid=(PAIRS,),
        in_specs=[
            columns(0),
            columns(PAIRS),
            columns(2 * PAIRS),
            pl.BlockSpec((2, SEQ, SEQ), lambda p: (p, 0, 0)),
        ],
        out_specs=[columns(0), pl.BlockSpec((2, SEQ, SEQ), lambda p: (p, 0, 0))],
        out_shape=[
            jax.ShapeDtypeStruct((SEQ, HEADS * DH), BF16),
            jax.ShapeDtypeStruct((HEADS, SEQ, SEQ), BF16),
        ],
        compiler_params=pltpu.CompilerParams(vmem_limit_bytes=VMEM_BYTES),
        cost_estimate=pl.CostEstimate(
            flops=ATTEND_COST,
            bytes_accessed=HEADS * SEQ * SEQ * 6,
            transcendentals=HEADS * SEQ * SEQ,
        ),
    )(packed, packed, packed, bias)


def attend_back_kernel(q_ref, k_ref, v_ref, grad_ref, prob_ref, out_ref, diag_ref, raw_ref, shift_ref):
    pair = pl.program_id(0)
    keys = k_ref[...]
    values = v_ref[...]
    query = q_ref[...]
    grads = grad_ref[...]
    masks = half_masks(ROWS)
    full_mask = half_masks(SEQ)[0]
    grad_query = [[None] * (SEQ // ROWS) for head in range(2)]
    grad_key = []
    grad_value = []
    for head in range(2):
        shift_ref[...] = jnp.zeros_like(shift_ref)
        for block in range(SEQ // ROWS):
            rows = slice(block * ROWS, (block + 1) * ROWS)
            grad_rows = grad_ref[rows, :]
            own = jnp.where(masks[head], grad_rows, jnp.zeros_like(grad_rows))
            grad_prob = dot_nt(own, values)
            prob = prob_ref[head, rows, :].astype(F32)
            weighted = prob * grad_prob
            grad_scores = weighted - prob * jnp.sum(weighted, axis=-1, keepdims=True)
            start = SEQ - ROWS * (block + 1)
            shift_ref[:, start : start + SEQ] += grad_scores
            raw = (grad_scores * DH ** (-0.5)).astype(BF16)
            raw_ref[rows, :] = raw
            grad_query[head][block] = jnp.dot(raw, keys, preferred_element_type=F32)
        grad_key.append(dot_tn(raw_ref[...], query))
        grad_value.append(dot_tn(prob_ref[head], grads))
        total = shift_ref[0:8, :]
        for group in range(1, ROWS // 8):
            total = total + pltpu.roll(
                shift_ref[8 * group : 8 * group + 8, :], SPAN - 8 * group, 1
            )
        diag_ref[0, head] = total
    width = 2 * DH

    def put(base, rows, value):
        spot = pl.multiple_of((base + pair) * width, width)
        out_ref[rows, pl.ds(spot, width)] = value.astype(BF16)

    for block in range(SEQ // ROWS):
        rows = slice(block * ROWS, (block + 1) * ROWS)
        put(0, rows, jnp.where(masks[0], grad_query[0][block], grad_query[1][block]))
    everything = slice(0, SEQ)
    put(PAIRS, everything, jnp.where(full_mask, grad_key[0], grad_key[1]))
    put(2 * PAIRS, everything, jnp.where(full_mask, grad_value[0], grad_value[1]))


def attend_backward(packed, grad_mixed, prob):
    def columns(base):
        return pl.BlockSpec((SEQ, 2 * DH), lambda p: (0, base + p))

    width = 3 * HEADS * DH
    return pl.pallas_call(
        attend_back_kernel,
        grid=(PAIRS,),
        in_specs=[
            columns(0),
            columns(PAIRS),
            columns(2 * PAIRS),
            columns(0),
            pl.BlockSpec((2, SEQ, SEQ), lambda p: (p, 0, 0)),
        ],
        out_specs=[
            pl.BlockSpec((SEQ, width), lambda p: (0, 0)),
            pl.BlockSpec((1, 2, 8, SPAN), lambda p: (p, 0, 0, 0)),
        ],
        out_shape=[
            jax.ShapeDtypeStruct((SEQ, width), BF16),
            jax.ShapeDtypeStruct((PAIRS, 2, 8, SPAN), F32),
        ],
        scratch_shapes=[pltpu.VMEM((SEQ, SEQ), BF16), pltpu.VMEM((ROWS, SPAN), F32)],
        compiler_params=pltpu.CompilerParams(vmem_limit_bytes=VMEM_BYTES),
        cost_estimate=pl.CostEstimate(
            flops=ATTEND_COST,
            bytes_accessed=HEADS * SEQ * SEQ * 2 + SEQ * width * 4,
            transcendentals=0,
        ),
    )(packed, packed, packed, grad_mixed, prob)


def bias_grad(diagonals):
    columns = jnp.arange(SPAN, dtype=jnp.int32)[None, :]
    offsets = columns - jnp.arange(8, dtype=jnp.int32)[:, None] - (SEQ - ROWS)
    offsets = jnp.where(offsets >= SEQ, offsets - SPAN, offsets)
    table = (bucket_of(offsets)[:, :, None] == jnp.arange(BUCKETS, dtype=jnp.int32)).astype(F32)
    return jnp.einsum(
        "hs,sb->bh",
        diagonals.reshape(HEADS, 8 * SPAN),
        table.reshape(8 * SPAN, BUCKETS),
        precision=PRECISE,
    )


def attention_forward(stream, gain_row, qkv_full, out_full, bias):
    normed_low = norm_scale(stream, gain_row.astype(F32)).astype(BF16)
    packed_low = jnp.dot(normed_low, qkv_full, preferred_element_type=F32).astype(BF16)
    mixed_low, prob_low = attend_forward(packed_low, bias)
    stream_after = stream + jnp.dot(mixed_low, out_full, preferred_element_type=F32)
    return (normed_low, packed_low, mixed_low, prob_low, stream_after)


def attention_back_in(grad_stream, out_full, kept_state):
    grad_low = grad_stream.astype(BF16)
    grad_out_w = jnp.einsum("td,te->de", kept_state[2], grad_low, preferred_element_type=F32)
    grad_mixed = jnp.einsum("te,de->td", grad_low, out_full, preferred_element_type=F32)
    return (grad_mixed.astype(BF16), grad_out_w.astype(BF16))


def attention_back_out(packed_grad, grad_stream, stream, gain_row, qkv_full, kept_state):
    grad_normed = jnp.einsum("te,de->td", packed_grad, qkv_full, preferred_element_type=F32)
    grad_input, grad_gain = norm_backward(grad_normed, stream, gain_row)
    return (grad_stream + grad_input, grad_gain)


def qkv_weight_term(packed_grad, kept_state):
    return jnp.einsum("td,te->de", kept_state[0], packed_grad, preferred_element_type=F32).astype(BF16)


def dense_forward(stream, gain_row, weight_in, weight_out):
    normed_low = norm_scale(stream, gain_row.astype(jnp.float32)).astype(jnp.bfloat16)
    hidden_pre = jnp.dot(normed_low, weight_in, preferred_element_type=jnp.float32)
    hidden_low = gelu_tanh(hidden_pre).astype(jnp.bfloat16)
    stream_after = stream + jnp.dot(hidden_low, weight_out, preferred_element_type=jnp.float32)
    return (normed_low, hidden_pre, stream_after)


def dense_back_in(grad_stream, weight_out, kept_state):
    grad_low = grad_stream.astype(jnp.bfloat16)
    gelu_value, gelu_pull = jax.vjp(gelu_tanh, kept_state[1])
    hidden_low = gelu_value.astype(jnp.bfloat16)
    grad_hidden = (
        jnp.einsum("td,fd->tf", grad_low, weight_out, preferred_element_type=jnp.float32)
        .astype(jnp.bfloat16)
        .astype(jnp.float32)
    )
    grad_pre = gelu_pull(grad_hidden)[0].astype(jnp.bfloat16)
    return (hidden_low, grad_low, grad_pre)


def dense_back_out(
    grad_stream, stream, gain_row, weight_in, hidden_low, grad_low, grad_pre, kept_state
):
    grad_w_out = jnp.einsum("tf,td->fd", hidden_low, grad_low, preferred_element_type=jnp.float32)
    grad_w_in = jnp.einsum("td,tf->df", kept_state[0], grad_pre, preferred_element_type=jnp.float32)
    grad_normed = jnp.einsum("tf,df->td", grad_pre, weight_in, preferred_element_type=jnp.float32)
    grad_input, grad_gain = norm_backward(grad_normed, stream, gain_row)
    return (
        grad_stream + grad_input,
        grad_gain,
        grad_w_in.astype(jnp.bfloat16),
        grad_w_out.astype(jnp.bfloat16),
    )


def dispatch_table(expert_ids, slot_ids, expert_count, capacity):
    target = jnp.where(slot_ids < capacity, expert_ids * capacity + slot_ids, -1)
    return (
        target[:, None] == jnp.arange(expert_count * capacity, dtype=jnp.int32)[None, :]
    ).astype(jnp.bfloat16)


def expert_forward(received, weight_in, weight_out):
    hidden_pre = jnp.einsum(
        "secd,edf->secf", received, weight_in, preferred_element_type=jnp.float32
    )
    hidden_low = gelu_tanh(hidden_pre).astype(jnp.bfloat16)
    produced = jnp.einsum(
        "secf,efd->secd", hidden_low, weight_out, preferred_element_type=jnp.float32
    )
    return (produced.astype(jnp.bfloat16), hidden_pre, received)


def sparse_forward(
    stream, gain_row, router_full, in_full, out_experts, expert_ids, slot_ids, expert_count
):
    normed_low = norm_scale(stream, gain_row.astype(jnp.float32)).astype(jnp.bfloat16)
    logits = jnp.dot(normed_low, router_full, preferred_element_type=jnp.float32)
    chosen = (expert_ids[:, None] == jnp.arange(expert_count, dtype=jnp.int32)[None, :]).astype(
        jnp.float32
    )
    gate_values = gate_of(logits, chosen)
    capacity = stream.shape[0] // expert_count
    slot_table = dispatch_table(expert_ids, slot_ids, expert_count, capacity)
    outgoing = jnp.einsum(
        "ts,td->sd", slot_table, normed_low, preferred_element_type=jnp.float32
    ).astype(jnp.bfloat16)
    outgoing = outgoing.reshape(expert_count // in_full.shape[0], in_full.shape[0], capacity, -1)
    produced, hidden_pre, received = expert_forward(
        lax.all_to_all(outgoing, EXPERT_AXES, split_axis=0, concat_axis=0, tiled=True),
        in_full,
        out_experts,
    )
    returned = lax.all_to_all(produced, EXPERT_AXES, split_axis=0, concat_axis=0, tiled=True)
    combined = jnp.dot(
        slot_table,
        returned.reshape(expert_count * capacity, -1),
        preferred_element_type=jnp.float32,
    )
    stream_after = stream + gate_values[:, None] * combined
    return (
        (normed_low, logits, chosen, gate_values, slot_table, combined, hidden_pre, received),
        stream_after,
    )


def sparse_backward(grad_stream, stream, gain_row, router_full, in_full, out_experts, kept_state):
    normed_low, logits, chosen, gate_values, slot_table, combined, hidden_pre, received = kept_state
    grad_gates = jnp.sum(grad_stream * combined, axis=-1)
    grad_combined = (gate_values[:, None] * grad_stream).astype(jnp.bfloat16)
    outgoing = jnp.einsum(
        "ts,td->sd", slot_table, grad_combined, preferred_element_type=jnp.float32
    ).astype(jnp.bfloat16)
    grad_produced = lax.all_to_all(
        outgoing.reshape(received.shape), EXPERT_AXES, split_axis=0, concat_axis=0, tiled=True
    )
    gelu_value, gelu_pull = jax.vjp(gelu_tanh, hidden_pre)
    hidden_low = gelu_value.astype(jnp.bfloat16)
    grad_w_out = jnp.einsum(
        "secf,secd->efd", hidden_low, grad_produced, preferred_element_type=jnp.float32
    )
    grad_hidden = (
        jnp.einsum("secd,efd->secf", grad_produced, out_experts, preferred_element_type=jnp.float32)
        .astype(jnp.bfloat16)
        .astype(jnp.float32)
    )
    grad_pre = gelu_pull(grad_hidden)[0].astype(jnp.bfloat16)
    grad_w_in = jnp.einsum("secd,secf->edf", received, grad_pre, preferred_element_type=jnp.float32)
    grad_received = jnp.einsum(
        "secf,edf->secd", grad_pre, in_full, preferred_element_type=jnp.float32
    ).astype(jnp.bfloat16)
    grad_sent = lax.all_to_all(grad_received, EXPERT_AXES, split_axis=0, concat_axis=0, tiled=True)
    grad_normed = jnp.dot(
        slot_table, grad_sent.reshape(slot_table.shape[1], -1), preferred_element_type=jnp.float32
    )
    gate_again, gate_pull = jax.vjp(gate_of, logits, chosen)
    grad_logits = gate_pull(grad_gates)[0].astype(jnp.bfloat16)
    grad_router = jnp.einsum(
        "td,te->de", normed_low, grad_logits, preferred_element_type=jnp.float32
    )
    grad_normed = grad_normed + jnp.einsum(
        "te,de->td", grad_logits, router_full, preferred_element_type=jnp.float32
    )
    grad_input, grad_gain = norm_backward(grad_normed, stream, gain_row)
    return (grad_stream + grad_input, grad_gain, grad_router, grad_w_in, grad_w_out)


def on_device(
    tokens_in,
    segment_ids,
    expert_index,
    expert_slot,
    attn_gain,
    qkv_weight,
    out_weight,
    rel_bias,
    ffn_gain,
    ffn_in,
    ffn_out,
    router,
    expert_in,
    expert_out,
    cotangent,
):
    width = tokens_in.shape[1]
    packed_width = qkv_weight.shape[2]
    expert_count = router.shape[1]
    small = jnp.concatenate([attn_gain.T, ffn_gain.T, router], axis=1)
    small_width = -(-small.shape[1] // 128) * 128
    small = jnp.pad(small, ((0, 0), (0, small_width - small.shape[1])))
    joined = packed_width + width
    hidden_width = ffn_in.shape[1]
    rows = ffn_in.shape[0]
    stack = ffn_out.shape[0] // rows
    first_shard = jnp.concatenate([qkv_weight[:, 0], out_weight[:, 0], small], axis=1)
    last_shard = jnp.concatenate([qkv_weight[:, 1], out_weight[:, 1]], axis=1)
    dense_shard = jnp.concatenate(
        [ffn_in] + [ffn_out[i * rows : (i + 1) * rows] for i in range(stack)], axis=1
    )
    first_line = gather_z(first_shard)
    first_line, dense_shard, last_shard, expert_in, expert_out = together(
        first_line, dense_shard, last_shard, expert_in, expert_out
    )
    in_full = lax.all_gather(expert_in, DATA_AXES, axis=1, tiled=True)
    out_experts = lax.all_gather(expert_out, DATA_AXES, axis=1, tiled=True)
    first_half = gather_across(first_line)
    dense_line = gather_z(dense_shard)
    first_half, dense_line = together(first_half, dense_line)
    qkv_zero, out_zero, small_full = gather_core(
        first_half,
        (((0, packed_width),), ((packed_width, joined),), ((joined, joined + small_width),)),
    )
    last_line = gather_z(last_shard)
    dense_half = gather_across(dense_line)
    dense_half, last_line = together(dense_half, last_line)
    ffn_in_full, ffn_out_full = gather_core(
        dense_half,
        (
            ((0, hidden_width),),
            tuple((hidden_width + i * width, hidden_width + (i + 1) * width) for i in range(stack)),
        ),
    )
    last_half = gather_across(last_line)
    qkv_one, out_one = gather_core(last_half, (((0, packed_width),), ((packed_width, joined),)))
    gains = small_full[:, :4].T
    router_full = small_full[:, 4 : 4 + expert_count]
    bias = masked_bias(rel_bias, segment_ids)

    stream_zero = tokens_in.astype(F32)
    attn_zero = attention_forward(stream_zero, gains[0], qkv_zero, out_zero, bias)
    dense_zero = dense_forward(attn_zero[4], gains[2], ffn_in_full, ffn_out_full)
    attn_one = attention_forward(dense_zero[2], gains[1], qkv_one, out_one, bias)
    sparse_one, stream_two = sparse_forward(
        attn_one[4],
        gains[3],
        router_full,
        in_full,
        out_experts,
        expert_index,
        expert_slot,
        expert_count,
    )

    grad_top = cotangent.astype(F32)
    grad_middle, ffn_gain_one, router_term, expert_in_term, expert_out_term = sparse_backward(
        grad_top, attn_one[4], gains[3], router_full, in_full, out_experts, sparse_one
    )
    expert_out_sum = lax.psum_scatter(
        expert_out_term.astype(BF16), DATA_AXES, scatter_dimension=1, tiled=True
    ).astype(F32)
    expert_in_sum = lax.psum_scatter(
        expert_in_term.astype(BF16), DATA_AXES, scatter_dimension=1, tiled=True
    ).astype(F32)

    grad_mixed_one, out_one_term = attention_back_in(grad_middle, out_one, attn_one)
    packed_grad_one, pairs_one = attend_backward(attn_one[1], grad_mixed_one, attn_one[3])
    qkv_one_term = qkv_weight_term(packed_grad_one, attn_one)
    grad_one, attn_gain_one = attention_back_out(
        packed_grad_one, grad_middle, dense_zero[2], gains[1], qkv_one, attn_one
    )
    last_half = scatter_core([(qkv_one_term, 1), (out_one_term, 1)])

    hidden_low, grad_low, grad_pre = dense_back_in(grad_one, ffn_out_full, dense_zero)
    last_half, grad_pre = together(last_half, grad_pre)
    last_line = scatter_across(last_half)
    grad_half, ffn_gain_zero, ffn_in_term, ffn_out_term = dense_back_out(
        grad_one, attn_zero[4], gains[2], ffn_in_full, hidden_low, grad_low, grad_pre, dense_zero
    )
    dense_half = scatter_core([(ffn_in_term, 1), (ffn_out_term, stack)])
    grad_mixed_zero, out_zero_term = attention_back_in(grad_half, out_zero, attn_zero)
    dense_half, grad_mixed_zero = together(dense_half, grad_mixed_zero)
    dense_line = scatter_across(dense_half)
    packed_grad_zero, pairs_zero = attend_backward(attn_zero[1], grad_mixed_zero, attn_zero[3])
    last_line, packed_grad_zero = together(last_line, packed_grad_zero)
    one_sum = scatter_z(last_line)
    qkv_zero_term = qkv_weight_term(packed_grad_zero, attn_zero)
    first_half = scatter_core([(qkv_zero_term, 1), (out_zero_term, 1)])
    grad_zero, attn_gain_zero = attention_back_out(
        packed_grad_zero, grad_half, stream_zero, gains[0], qkv_zero, attn_zero
    )
    first_half, grad_zero, dense_line = together(first_half, grad_zero, dense_line)
    first_line = scatter_across(first_half)
    dense_sum = scatter_z(dense_line)
    zero_sum = scatter_z(first_line)
    ffn_in_sum = dense_sum[:, :hidden_width]
    ffn_out_sum = jnp.concatenate(
        [dense_sum[:, hidden_width + i * width : hidden_width + (i + 1) * width] for i in range(stack)]
    )
    qkv_sum = jnp.stack([zero_sum[:, :packed_width], one_sum[:, :packed_width]], axis=1)
    out_sum = jnp.stack([zero_sum[:, packed_width:], one_sum[:, packed_width:]], axis=1)

    bias_term = bias_grad(pairs_zero + pairs_one)
    tiny = jnp.concatenate(
        [
            attn_gain_zero,
            attn_gain_one,
            ffn_gain_zero,
            ffn_gain_one,
            router_term.reshape(-1),
            bias_term.reshape(-1),
        ]
    )
    tiny_sum = sum_everywhere(tiny.reshape(-1, 128)).reshape(-1)
    gain_sums = tiny_sum[: 4 * width].reshape(4, width)
    router_sums = tiny_sum[4 * width : (4 + expert_count) * width].reshape(width, expert_count)
    bias_sum = tiny_sum[(4 + expert_count) * width :].reshape(BUCKETS, HEADS)
    first_row = lax.axis_index(ALL_AXES) * rows
    gain_shard = lax.dynamic_slice_in_dim(gain_sums, first_row, rows, 1)
    router_shard = lax.dynamic_slice_in_dim(router_sums, first_row, rows, 0)
    return (
        stream_two.astype(BF16),
        grad_zero,
        gain_shard[:2],
        qkv_sum,
        out_sum,
        bias_sum,
        gain_shard[2:],
        ffn_in_sum,
        ffn_out_sum,
        router_shard,
        expert_in_sum,
        expert_out_sum,
    )


def solution(mesh):
    experts, data = mesh.shape["expert"], mesh.shape["dp"]
    side = 1 << ((experts.bit_length() - 1) // 2)
    fine = Mesh(mesh.devices.reshape(experts // side, side, data // 2, 2), ALL_AXES)
    placed = (
        P(ALL_AXES, None),
        P(ALL_AXES, None),
        P(ALL_AXES),
        P(ALL_AXES),
        P(None, ALL_AXES),
        P(ALL_AXES, None, None),
        P(ALL_AXES, None, None),
        P(),
        P(None, ALL_AXES),
        P(ALL_AXES, None),
        P(ALL_AXES, None),
        P(ALL_AXES, None),
        P(EXPERT_AXES, DATA_AXES, None),
        P(EXPERT_AXES, DATA_AXES, None),
        P(ALL_AXES, None),
    )
    return jax.shard_map(
        on_device,
        mesh=fine,
        in_specs=placed,
        out_specs=(
            P(ALL_AXES, None),
            P(ALL_AXES, None),
            P(None, ALL_AXES),
            P(ALL_AXES, None, None),
            P(ALL_AXES, None, None),
            P(),
            P(None, ALL_AXES),
            P(ALL_AXES, None),
            P(ALL_AXES, None),
            P(ALL_AXES, None),
            P(EXPERT_AXES, DATA_AXES, None),
            P(EXPERT_AXES, DATA_AXES, None),
        ),
        check_vma=False,
    )
```

time: 1220 us -> 657 us (0.54)
  waiting for transfers between devices: 662 us -> 224 us
  blocking collectives: 173 us -> 15.5 us
  matrix products: 256 us -> 109 us
  Pallas kernels: 0 us -> 116 us
  starting transfers between devices: 11.9 us -> 84 us
  local copies, waits for them, and re-layouts: 65.8 us -> 51.3 us
    reduce_scatter x6 -> x2, waiting for transfers between devices: 466 us -> 0.02 us  [the longest x1 0.02 us: on_device(): lax.psum_scatter(expert_out_term.astype(BF16), DATA_AXES, scatter_dimensi...]
    ppermute x0 -> x49, waiting for transfers between devices: none -> 200 us  [swap_with(): return lax.ppermute(value, axes, [(i, i ^ flip) for i in range(count)])]
    all_gather x6 -> x2, waiting for transfers between devices: 184 us -> 0.01 us  [the longest x1 0.01 us: on_device(): in_full = lax.all_gather(expert_in, DATA_AXES, axis=1, tiled=True)]
    all_gather x3 -> x0, blocking collectives: 120 us -> none  [the longest x1 43.3 us: on_device(): lax.all_gather(attn_gain, ('expert', 'dp'), axis=1, tiled=True)]
    pallas_call x0 -> x14, Pallas kernels: none -> 116 us  [the longest x2 42.9 us: attend_forward(): pl.pallas_call(attend_kernel, grid=(PAIRS,), in_specs=[columns(0), column...]
    dot_general x28 -> x18, matrix products: 149 us -> 45 us  [the longest x1 7.64 us: dense_back_in(): jnp.einsum('td,fd->tf', grad_low, weight_out, preferred_element_type=jnp....]
    ppermute x0 -> x49, starting transfers between devices: none -> 70.8 us  [swap_with(): return lax.ppermute(value, axes, [(i, i ^ flip) for i in range(count)])]
    sub x2 -> x0, matrix products: 43.1 us -> none  [one_block(): grad_weights - jnp.sum(weights_now * grad_weights, axis=-1, keepdims=True)]
  transfers between devices with their start and end apart: 15 -> 56, of which waited for: 9 -> 31; matrix products, arithmetic and copies ran while one was open for 21% -> 21% of each run, Pallas kernels for 0% -> 18%
where the time goes in v1:
time: 657 us; the launch traced here: 647 us
  waiting for transfers between devices  224 us (34%)
  Pallas kernels  116 us (18%)
  matrix products  109 us (17%)
  starting transfers between devices  84 us (13%)
  local copies, waits for them, and re-layouts  51.3 us (8%)
  other arithmetic  30.5 us (5%)
  between operations  15.6 us (2%)
  blocking collectives  15.5 us (2%)
    ppermute x49, waiting for transfers between devices, swap_with(): return lax.ppermute(value, axes, [(i, i ^ flip) for i in range(count)])  200 us
    ppermute x49, starting transfers between devices, swap_with(): return lax.ppermute(value, axes, [(i, i ^ flip) for i in range(count)])  70.8 us
    pallas_call x2, Pallas kernels, attend_forward(): pl.pallas_call(attend_kernel, grid=(PAIRS,), in_specs=[columns(0), column...  42.9 us
    pallas_call x2, Pallas kernels, attend_backward(): pl.pallas_call(attend_back_kernel, grid=(PAIRS,), in_specs=[columns(0), c...  38.8 us
    unnamed x188, local copies, waits for them, and re-layouts  30.4 us
    pallas_call x9, Pallas kernels, place(): pl.pallas_call(functools.partial(place_kernel, len(parts), axis, groups),...  26.7 us
    all_to_all x1, blocking collectives, sparse_forward(): lax.all_to_all(outgoing, EXPERT_AXES, split_axis=0, concat_axis=0, tiled=...  15.5 us
  transfers between devices with their start and end apart: 56, of which 31 were waited for; matrix products, arithmetic and copies ran while one was open for 21% of the time, Pallas kernels for 18%

profile of v1, /device:TPU:0, one launch (start us, length us, event | category | flops | bytes accessed | tf_op | source)
XLA Modules:
  0.0 646.6 jit_solution(11714857799932911817)
XLA Ops:
  20.7 8.1 %collective-permute-done.1.refs_2_ = bf16[24,3200]{1,0:T(8,128)(2,1)S(1)} collective-permute-done((bf16[24,3200]{1,0:T(8,128)(2,1)S(1)}, bf16[24,3200]{1,0:T(8,128)(2,1)S(1)}, u32[]{:S(2)}, u32[]{:S(2)}) %collective-permute-start.1) | collective-permute-done | bytes 153632 | tf_op jit(solution)/shard_map/ppermute | solution.py:62
  36.5 12.3 %collective-permute-done.8.refs_3_ = bf16[24,6144]{1,0:T(8,128)(2,1)S(1)} collective-permute-done((bf16[24,6144]{1,0:T(8,128)(2,1)S(1)}, bf16[24,6144]{1,0:T(8,128)(2,1)S(1)}, u32[]{:S(2)}, u32[]{:S(2)}) %collective-permute-start.8) | collective-permute-done | bytes 294944 | tf_op jit(solution)/shard_map/ppermute | solution.py:62
  48.9 23.2 %collective-permute-start.6 = (bf16[24,6144]{1,0:T(8,128)(2,1)S(1)}, bf16[24,6144]{1,0:T(8,128)(2,1)}, u32[]{:S(2)}, u32[]{:S(2)}) collective-permute-start(bf16[24,6144]{1,0:T(8,128)(2,1)S(1)} %slice_dynamic-update-slice_fusion.refs_0_), channel_id=1, source_target_pairs={{0,2},{2,0},{4,6},{6,4},{1,3},{3,1},{5,7},{7,5},{8,10},{10,8},{12,... | collective-permute-start | bytes 884744 | tf_op jit(solution)/shard_map/ppermute | solution.py:62
  72.0 15.6 %collective-permute-done.7.refs_2_ = bf16[24,6144]{1,0:T(8,128)(2,1)S(1)} collective-permute-done((bf16[24,6144]{1,0:T(8,128)(2,1)S(1)}, bf16[24,6144]{1,0:T(8,128)(2,1)S(1)}, u32[]{:S(2)}, u32[]{:S(2)}) %collective-permute-start.7) | collective-permute-done | bytes 294944 | tf_op jit(solution)/shard_map/ppermute | solution.py:62
  128.3 9.4 %collective-permute-done.11.refs_2_ = bf16[4,24,6144]{2,1,0:T(8,128)(2,1)} collective-permute-done((bf16[4,24,6144]{2,1,0:T(8,128)(2,1)}, bf16[4,24,6144]{2,1,0:T(8,128)(2,1)}, u32[]{:S(2)}, u32[]{:S(2)}) %collective-permute-start.11) | collective-permute-done | bytes 1179680 | tf_op jit(solution)/shard_map/ppermute | solution.py:62
  147.5 8.1 %shard_map.242.bias_ref = f32[12,512,512]{2,1,0:T(8,128)} custom-call(f32[12,1,1024]{2,1,0:T(1,128)S(1)} %reshape.377.row_ref, s32[512,1]{1,0:T(8,128)S(1)} %copy.102.seg_col_ref, s32[1,512]{1,0:T(1,128)S(1)} %copy-done.13), custom_call_target="tpu_custom_call" | custom-call | flops 7333333504 | bytes 25165824 | tf_op jit(solution)/shard_map/pallas_call | solution.py:206
  161.1 12.2 %collective-permute-done.18.refs_2_ = bf16[4,24,3072]{2,1,0:T(8,128)(2,1)} collective-permute-done((bf16[4,24,3072]{2,1,0:T(8,128)(2,1)S(1)}, bf16[4,24,3072]{2,1,0:T(8,128)(2,1)}, u32[]{:S(2)}, u32[]{:S(2)}) %collective-permute-start.18) | collective-permute-done | bytes 589856 | tf_op jit(solution)/shard_map/ppermute | solution.py:62
  185.5 21.5 %shard_map.243 = (bf16[512,768]{1,0:T(8,128)(2,1)S(1)}, bf16[12,512,512]{2,1,0:T(8,128)(2,1)}) custom-call(bf16[512,2304]{1,0:T(8,128)(2,1)S(1)} %convolution_convert_fusion.6.q_ref.k_ref.v_ref, bf16[512,2304]{1,0:T(8,128)(2,1)S(1)} %convolution_convert_fusion.6.q_ref.k_ref.v_ref, bf16[512,2304]{1,0:T(8,128)(2,1)S(1)} %convolution_convert_fusion.6.q_ref.k_ref.v_ref, ...), custom_call_target="tpu_custom_call" | custom-call | flops 22000001024 | bytes 18874368 | tf_op jit(solution)/shard_map/pallas_call | solution.py:259
  231.3 21.4 %shard_map.249 = (bf16[512,768]{1,0:T(8,128)(2,1)S(1)}, bf16[12,512,512]{2,1,0:T(8,128)(2,1)}) custom-call(bf16[512,2304]{1,0:T(8,128)(2,1)S(1)} %convolution_convert_fusion.5.q_ref.k_ref.v_ref, bf16[512,2304]{1,0:T(8,128)(2,1)S(1)} %convolution_convert_fusion.5.q_ref.k_ref.v_ref, bf16[512,2304]{1,0:T(8,128)(2,1)S(1)} %convolution_convert_fusion.5.q_ref.k_ref.v_ref, ...), custom_call_target="tpu_custom_call" | custom-call | flops 22000001024 | bytes 18874368 | tf_op jit(solution)/shard_map/pallas_call | solution.py:259
  255.6 15.5 %all_to_all.20 = bf16[4,1,128,768]{3,2,1,0:T(8,128)(2,1)} all-to-all(bf16[4,1,128,768]{3,2,1,0:T(8,128)(2,1)S(1)} %bitcast.358), channel_id=1, replica_groups=mesh['ey'=2,'ex'=2,'z'=4,'core'=2] {'ey','ex'}, dimensions={0} | all-to-all | bytes 1572864 | tf_op jit(solution)/shard_map/all_to_all | solution.py:471
  278.2 7.8 %fusion.71 = bf16[4,1,128,768]{2,3,1,0:T(8,128)(2,1)} fusion(bf16[1,3072,768]{1,2,0:T(8,128)(2,1)} %all-gather.3.cloned.1.call-done, f32[3072,4,128]{2,0,1:T(8,128)} %fusion.25), kind=kOutput, calls=%fused_computation.119 | convolution fusion | flops 2430468096 | bytes 11796480 | tf_op jit(solution)/shard_map/secf,efd->secd/dot_general | solution.py:449
  290.7 10.3 %all-to-all-done.1 = bf16[4,1,128,768]{2,3,1,0:T(8,128)(2,1)} async-done(((bf16[4,1,128,768]{2,3,1,0:T(8,128)(2,1)}), bf16[4,1,128,768]{2,3,1,0:T(8,128)(2,1)}, u32[]{:S(2)}, u32[]{:S(2)}) %all-to-all-start.1) | async-done | bytes 786464 | tf_op jit(solution)/shard_map/all_to_all | solution.py:475
  312.9 10.3 %all-to-all-done.2 = bf16[4,1,128,768]{3,2,1,0:T(8,128)(2,1)} async-done(((bf16[4,1,128,768]{3,2,1,0:T(8,128)(2,1)}), bf16[4,1,128,768]{3,2,1,0:T(8,128)(2,1)}, u32[]{:S(2)}, u32[]{:S(2)}) %all-to-all-start.2) | async-done | bytes 786464 | tf_op jit(solution)/shard_map/all_to_all | solution.py:495
  323.2 9.7 %fusion.16 = bf16[4,1,128,3072]{2,3,0,1:T(8,128)(2,1)S(1)} fusion(f32[3072,4,128]{2,0,1:T(8,128)} %fusion.25, bf16[1,3072,768]{1,2,0:T(8,128)(2,1)} %all-gather.3.cloned.1.call-done, bf16[4,1,128,768]{3,2,1,0:T(8,128)(2,1)} %all-to-all-done.2), kind=kOutput, calls=%fused_computation.25 | convolution fusion | flops 2450522112 | bytes 14942208 | tf_op jit(solution)/shard_map/secd,efd->secf/dot_general | solution.py:504
  363.7 19.4 %shard_map.250 = (bf16[512,2304]{1,0:T(8,128)(2,1)S(1)}, f32[6,2,8,1024]{3,2,1,0:T(8,128)S(1)}) custom-call(bf16[512,2304]{1,0:T(8,128)(2,1)S(1)} %copy-done.18, bf16[512,2304]{1,0:T(8,128)(2,1)S(1)} %copy-done.18, bf16[512,2304]{1,0:T(8,128)(2,1)S(1)} %copy-done.18, bf16[512,768]{1,0:T(8,128)(2,1)S(1)} %convolution_convert_fusion.10.grad_ref, ...), custom_call_target="tpu_custom_call" | custom-call | flops 22000001024 | bytes 11010048 | tf_op jit(solution)/shard_map/pallas_call | solution.py:335
  395.9 7.6 %fusion.2 = bf16[512,3072]{1,0:T(8,128)(2,1)S(1)} fusion(f32[512,3072]{1,0:T(8,128)S(1)} %bitcast.345, bf16[3072,768]{1,0:T(8,128)(2,1)} %bitcast.367, f32[512,768]{1,0:T(8,128)S(1)} %fusion.51), kind=kOutput, calls=%fused_computation.11 | convolution fusion | flops 2450915328 | bytes 15728640 | tf_op jit(solution)/shard_map/td,fd->tf/dot_general | solution.py:414
  444.6 13.3 %collective-permute-done.24 = bf16[4,24,3072]{2,1,0:T(8,128)(2,1)S(1)} collective-permute-done((bf16[4,24,3072]{2,1,0:T(8,128)(2,1)S(1)}, bf16[4,24,3072]{2,1,0:T(8,128)(2,1)S(1)}, u32[]{:S(2)}, u32[]{:S(2)}) %collective-permute-start.24) | collective-permute-done | bytes 589856 | tf_op jit(solution)/shard_map/ppermute | solution.py:62
  460.5 8.2 %add_convert_fusion = bf16[16,24,6144]{2,1,0:T(8,128)(2,1)} fusion(bf16[16,24,6144]{2,1,0:T(8,128)(2,1)} %collective-permute-done.25, bf16[16,24,6144]{2,1,0:T(8,128)(2,1)} %get-tuple-element.166), kind=kLoop, calls=%fused_computation.2 | loop fusion | flops 9437184 | bytes 14155776 | tf_op jit(solution)/shard_map/convert_element_type | solution.py:170
  468.6 19.4 %shard_map.251 = (bf16[512,2304]{1,0:T(8,128)(2,1)S(1)}, f32[6,2,8,1024]{3,2,1,0:T(8,128)S(1)}) custom-call(bf16[512,2304]{1,0:T(8,128)(2,1)S(1)} %copy-done.20, bf16[512,2304]{1,0:T(8,128)(2,1)S(1)} %copy-done.20, bf16[512,2304]{1,0:T(8,128)(2,1)S(1)} %copy-done.20, bf16[512,768]{1,0:T(8,128)(2,1)S(1)} %convolution_convert_fusion.9.grad_ref, ...), custom_call_target="tpu_custom_call" | custom-call | flops 22000001024 | bytes 11010048 | tf_op jit(solution)/shard_map/pallas_call | solution.py:335
  524.7 20.4 %collective-permute-done.27 = bf16[4,24,6144]{2,1,0:T(8,128)(2,1)S(1)} collective-permute-done((bf16[4,24,6144]{2,1,0:T(8,128)(2,1)}, bf16[4,24,6144]{2,1,0:T(8,128)(2,1)S(1)}, u32[]{:S(2)}, u32[]{:S(2)}) %collective-permute-start.27) | collective-permute-done | bytes 1179680 | tf_op jit(solution)/shard_map/ppermute | solution.py:62
  545.2 25.6 %collective-permute-done.29 = bf16[4,24,6144]{2,1,0:T(8,128)(2,1)S(1)} collective-permute-done((bf16[4,24,6144]{2,1,0:T(8,128)(2,1)}, bf16[4,24,6144]{2,1,0:T(8,128)(2,1)S(1)}, u32[]{:S(2)}, u32[]{:S(2)}) %collective-permute-start.29) | collective-permute-done | bytes 1179680 | tf_op jit(solution)/shard_map/ppermute | solution.py:62
  589.8 8.4 %collective-permute-done.46 = bf16[24,6144]{1,0:T(8,128)(2,1)S(1)} collective-permute-done((bf16[24,6144]{1,0:T(8,128)(2,1)S(1)}, bf16[24,6144]{1,0:T(8,128)(2,1)S(1)}, u32[]{:S(2)}, u32[]{:S(2)}) %collective-permute-start.46) | collective-permute-done | bytes 294944 | tf_op jit(solution)/shard_map/ppermute | solution.py:62
  599.0 13.0 %collective-permute-done.47 = bf16[24,6144]{1,0:T(8,128)(2,1)S(1)} collective-permute-done((bf16[24,6144]{1,0:T(8,128)(2,1)S(1)}, bf16[24,6144]{1,0:T(8,128)(2,1)S(1)}, u32[]{:S(2)}, u32[]{:S(2)}) %collective-permute-start.47) | collective-permute-done | bytes 294944 | tf_op jit(solution)/shard_map/ppermute | solution.py:62
  614.0 9.2 %collective-permute-done.38 = bf16[4,24,3072]{2,1,0:T(8,128)(2,1)S(1)} collective-permute-done((bf16[4,24,3072]{2,1,0:T(8,128)(2,1)S(1)}, bf16[4,24,3072]{2,1,0:T(8,128)(2,1)S(1)}, u32[]{:S(2)}, u32[]{:S(2)}) %collective-permute-start.38) | collective-permute-done | bytes 589856 | tf_op jit(solution)/shard_map/ppermute | solution.py:62
  (415 shorter events, 300.9 us)
Async XLA Ops:
  7.2 263.9 %all-gather.5.cloned.1.call-start = ((), (), s32[]{:S(2)}) async-start(), calls=%async_computation.7 | async-start | bytes 5308416 | tf_op jit(solution)/shard_map/all_gather | solution.py:565
  30.5 247.7 %all-gather.3.cloned.1.call-start = ((), (), s32[]{:S(2)}) async-start(), calls=%async_computation.6 | async-start | bytes 5308416 | tf_op jit(solution)/shard_map/all_gather | solution.py:566
  30.5 62.5 %collective-permute-start.5 = (bf16[4,24,3200]{2,1,0:T(8,128)(2,1)S(1)}, bf16[4,24,3200]{2,1,0:T(8,128)(2,1)S(1)}, u32[]{:S(2)}, u32[]{:S(2)}) collective-permute-start(bf16[4,24,3200]{2,1,0:T(8,128)(2,1)S(1)} %shard_map.238.refs_0_), channel_id=1, source_target_pairs={{0,24},{8,16},{16,8},{24,0},{1,25},{9,17},{17,9},{25,1},{2,26},{10... | collective-permute-start | bytes 1843208 | tf_op jit(solution)/shard_map/ppermute | solution.py:62
  33.0 60.9 %collective-permute-start.4 = (bf16[4,24,3200]{2,1,0:T(8,128)(2,1)S(1)}, bf16[4,24,3200]{2,1,0:T(8,128)(2,1)S(1)}, u32[]{:S(2)}, u32[]{:S(2)}) collective-permute-start(bf16[4,24,3200]{2,1,0:T(8,128)(2,1)S(1)} %shard_map.238.refs_0_), channel_id=1, source_target_pairs={{0,16},{8,24},{16,0},{24,8},{1,17},{9,25},{17,1},{25,9},{2,18},{10... | collective-permute-start | bytes 1843208 | tf_op jit(solution)/shard_map/ppermute | solution.py:62
  33.5 61.2 %collective-permute-start.3 = (bf16[4,24,3200]{2,1,0:T(8,128)(2,1)S(1)}, bf16[4,24,3200]{2,1,0:T(8,128)(2,1)S(1)}, u32[]{:S(2)}, u32[]{:S(2)}) collective-permute-start(bf16[4,24,3200]{2,1,0:T(8,128)(2,1)S(1)} %shard_map.238.refs_0_), channel_id=1, source_target_pairs={{0,8},{8,0},{16,24},{24,16},{1,9},{9,1},{17,25},{25,17},{2,10},{10... | collective-permute-start | bytes 1843208 | tf_op jit(solution)/shard_map/ppermute | solution.py:62
  36.5 51.1 %collective-permute-start.7 = (bf16[24,6144]{1,0:T(8,128)(2,1)S(1)}, bf16[24,6144]{1,0:T(8,128)(2,1)S(1)}, u32[]{:S(2)}, u32[]{:S(2)}) collective-permute-start(bf16[24,6144]{1,0:T(8,128)(2,1)S(1)} %slice_dynamic-update-slice_fusion.refs_0_), channel_id=1, source_target_pairs={{0,4},{2,6},{4,0},{6,2},{1,5},{3,7},{5,1},{7,3},{8,12},{10,14},{12... | collective-permute-start | bytes 884744 | tf_op jit(solution)/shard_map/ppermute | solution.py:62
  48.9 42.2 %collective-permute-start.6 = (bf16[24,6144]{1,0:T(8,128)(2,1)S(1)}, bf16[24,6144]{1,0:T(8,128)(2,1)}, u32[]{:S(2)}, u32[]{:S(2)}) collective-permute-start(bf16[24,6144]{1,0:T(8,128)(2,1)S(1)} %slice_dynamic-update-slice_fusion.refs_0_), channel_id=1, source_target_pairs={{0,2},{2,0},{4,6},{6,4},{1,3},{3,1},{5,7},{7,5},{8,10},{10,8},{12,... | collective-permute-start | bytes 884744 | tf_op jit(solution)/shard_map/ppermute | solution.py:62
  100.1 28.2 %collective-permute-start.12 = (bf16[4,24,6144]{2,1,0:T(8,128)(2,1)}, bf16[4,24,6144]{2,1,0:T(8,128)(2,1)}, u32[]{:S(2)}, u32[]{:S(2)}) collective-permute-start(bf16[4,24,6144]{2,1,0:T(8,128)(2,1)} %shard_map.240.refs_0_), channel_id=1, source_target_pairs={{0,24},{8,16},{16,8},{24,0},{1,25},{9,17},{17,9},{25,1},{2,26},{10... | collective-permute-start | bytes 3538952 | tf_op jit(solution)/shard_map/ppermute | solution.py:62
  102.6 35.1 %collective-permute-start.11 = (bf16[4,24,6144]{2,1,0:T(8,128)(2,1)}, bf16[4,24,6144]{2,1,0:T(8,128)(2,1)}, u32[]{:S(2)}, u32[]{:S(2)}) collective-permute-start(bf16[4,24,6144]{2,1,0:T(8,128)(2,1)} %shard_map.240.refs_0_), channel_id=1, source_target_pairs={{0,16},{8,24},{16,0},{24,8},{1,17},{9,25},{17,1},{25,9},{2,18},{10... | collective-permute-start | bytes 3538952 | tf_op jit(solution)/shard_map/ppermute | solution.py:62
  103.1 34.8 %collective-permute-start.10 = (bf16[4,24,6144]{2,1,0:T(8,128)(2,1)}, bf16[4,24,6144]{2,1,0:T(8,128)(2,1)}, u32[]{:S(2)}, u32[]{:S(2)}) collective-permute-start(bf16[4,24,6144]{2,1,0:T(8,128)(2,1)} %shard_map.240.refs_0_), channel_id=1, source_target_pairs={{0,8},{8,0},{16,24},{24,16},{1,9},{9,1},{17,25},{25,17},{2,10},{10... | collective-permute-start | bytes 3538952 | tf_op jit(solution)/shard_map/ppermute | solution.py:62
  103.6 72.5 %collective-permute-start.9 = (bf16[16,24,3200]{2,1,0:T(8,128)(2,1)S(1)}, bf16[16,24,3200]{2,1,0:T(8,128)(2,1)}, u32[]{:S(2)}, u32[]{:S(2)}) collective-permute-start(bf16[16,24,3200]{2,1,0:T(8,128)(2,1)S(1)} %bitcast.322), channel_id=1, source_target_pairs={{0,1},{1,0},{2,3},{3,2},{4,5},{5,4},{6,7},{7,6},{8,9},{9,8},{10,11... | collective-permute-start | bytes 7372808 | tf_op jit(solution)/shard_map/ppermute | solution.py:62
  141.7 70.5 %collective-permute-start.16 = (bf16[16,24,6144]{2,1,0:T(8,128)(2,1)}, bf16[16,24,6144]{2,1,0:T(8,128)(2,1)}, u32[]{:S(2)}, u32[]{:S(2)}) collective-permute-start(bf16[16,24,6144]{2,1,0:T(8,128)(2,1)} %bitcast.338), channel_id=1, source_target_pairs={{0,1},{1,0},{2,3},{3,2},{4,5},{5,4},{6,7},{7,6},{8,9},{9,8},{10,11... | collective-permute-start | bytes 14155784 | tf_op jit(solution)/shard_map/ppermute | solution.py:62
  145.5 27.9 %collective-permute-start.18 = (bf16[4,24,3072]{2,1,0:T(8,128)(2,1)S(1)}, bf16[4,24,3072]{2,1,0:T(8,128)(2,1)}, u32[]{:S(2)}, u32[]{:S(2)}) collective-permute-start(bf16[4,24,3072]{2,1,0:T(8,128)(2,1)S(1)} %shard_map.245.refs_0_), channel_id=1, source_target_pairs={{0,16},{8,24},{16,0},{24,8},{1,17},{9,25},{17,1},{25,9},{2,18},{10... | collective-permute-start | bytes 1769480 | tf_op jit(solution)/shard_map/ppermute | solution.py:62
  176.0 32.5 %collective-permute-start.20 = (bf16[16,24,3072]{2,1,0:T(8,128)(2,1)}, bf16[16,24,3072]{2,1,0:T(8,128)(2,1)}, u32[]{:S(2)}, u32[]{:S(2)}) collective-permute-start(bf16[16,24,3072]{2,1,0:T(8,128)(2,1)} %bitcast.19.refs_0_), channel_id=1, source_target_pairs={{0,1},{1,0},{2,3},{3,2},{4,5},{5,4},{6,7},{7,6},{8,9},{9,8},{10,11... | collective-permute-start | bytes 7077896 | tf_op jit(solution)/shard_map/ppermute | solution.py:62
  344.5 232.4 %reduce-scatter.5.cloned.1.call-start = ((), (), s32[]{:S(2)}) async-start(), calls=%async_computation.9 | async-start | bytes 5308416 | tf_op jit(solution)/shard_map/reduce_scatter | solution.py:609
  352.2 227.0 %reduce-scatter.3.cloned.1.call-start = ((), (), s32[]{:S(2)}) async-start(), calls=%async_computation.8 | async-start | bytes 5308416 | tf_op jit(solution)/shard_map/reduce_scatter | solution.py:612
  416.9 43.5 %collective-permute-start.25 = (bf16[16,24,6144]{2,1,0:T(8,128)(2,1)}, bf16[16,24,6144]{2,1,0:T(8,128)(2,1)}, u32[]{:S(2)}, u32[]{:S(2)}) collective-permute-start(bf16[16,24,6144]{2,1,0:T(8,128)(2,1)} %get-tuple-element.167), channel_id=1, source_target_pairs={{0,1},{1,0},{2,3},{3,2},{4,5},{5,4},{6,7},{7,6},{8,9},{9,8},{10,11... | collective-permute-start | bytes 14155784 | tf_op jit(solution)/shard_map/ppermute | solution.py:62
  429.9 28.0 %collective-permute-start.24 = (bf16[4,24,3072]{2,1,0:T(8,128)(2,1)S(1)}, bf16[4,24,3072]{2,1,0:T(8,128)(2,1)S(1)}, u32[]{:S(2)}, u32[]{:S(2)}) collective-permute-start(bf16[4,24,3072]{2,1,0:T(8,128)(2,1)S(1)} %get-tuple-element.157), channel_id=1, source_target_pairs={{0,24},{8,16},{16,8},{24,0},{1,25},{9,17},{17,9},{25,1},{2,26},{10... | collective-permute-start | bytes 1769480 | tf_op jit(solution)/shard_map/ppermute | solution.py:62
  431.5 27.8 %collective-permute-start.23 = (bf16[4,24,3072]{2,1,0:T(8,128)(2,1)S(1)}, bf16[4,24,3072]{2,1,0:T(8,128)(2,1)S(1)}, u32[]{:S(2)}, u32[]{:S(2)}) collective-permute-start(bf16[4,24,3072]{2,1,0:T(8,128)(2,1)S(1)} %get-tuple-element.158), channel_id=1, source_target_pairs={{0,16},{8,24},{16,0},{24,8},{1,17},{9,25},{17,1},{25,9},{2,18},{10... | collective-permute-start | bytes 1769480 | tf_op jit(solution)/shard_map/ppermute | solution.py:62
  516.2 65.2 %collective-permute-start.26 = (bf16[16,24,3072]{2,1,0:T(8,128)(2,1)}, bf16[16,24,3072]{2,1,0:T(8,128)(2,1)}, u32[]{:S(2)}, u32[]{:S(2)}) collective-permute-start(bf16[16,24,3072]{2,1,0:T(8,128)(2,1)} %pad_maximum_fusion.1), channel_id=1, source_target_pairs={{0,1},{1,0},{2,3},{3,2},{4,5},{5,4},{6,7},{7,6},{8,9},{9,8},{10,11... | collective-permute-start | bytes 7077896 | tf_op jit(solution)/shard_map/ppermute | solution.py:62
  516.2 29.0 %collective-permute-start.27 = (bf16[4,24,6144]{2,1,0:T(8,128)(2,1)}, bf16[4,24,6144]{2,1,0:T(8,128)(2,1)S(1)}, u32[]{:S(2)}, u32[]{:S(2)}) collective-permute-start(bf16[4,24,6144]{2,1,0:T(8,128)(2,1)} %get-tuple-element.140), channel_id=1, source_target_pairs={{0,8},{8,0},{16,24},{24,16},{1,9},{9,1},{17,25},{25,17},{2,10},{10... | collective-permute-start | bytes 3538952 | tf_op jit(solution)/shard_map/ppermute | solution.py:62
  519.9 50.9 %collective-permute-start.29 = (bf16[4,24,6144]{2,1,0:T(8,128)(2,1)}, bf16[4,24,6144]{2,1,0:T(8,128)(2,1)S(1)}, u32[]{:S(2)}, u32[]{:S(2)}) collective-permute-start(bf16[4,24,6144]{2,1,0:T(8,128)(2,1)} %get-tuple-element.141), channel_id=1, source_target_pairs={{0,24},{8,16},{16,8},{24,0},{1,25},{9,17},{17,9},{25,1},{2,26},{10... | collective-permute-start | bytes 3538952 | tf_op jit(solution)/shard_map/ppermute | solution.py:62
  521.4 53.3 %collective-permute-start.28 = (bf16[4,24,6144]{2,1,0:T(8,128)(2,1)}, bf16[4,24,6144]{2,1,0:T(8,128)(2,1)S(1)}, u32[]{:S(2)}, u32[]{:S(2)}) collective-permute-start(bf16[4,24,6144]{2,1,0:T(8,128)(2,1)} %get-tuple-element.142), channel_id=1, source_target_pairs={{0,16},{8,24},{16,0},{24,8},{1,17},{9,25},{17,1},{25,9},{2,18},{10... | collective-permute-start | bytes 3538952 | tf_op jit(solution)/shard_map/ppermute | solution.py:62
  584.0 28.1 %collective-permute-start.47 = (bf16[24,6144]{1,0:T(8,128)(2,1)S(1)}, bf16[24,6144]{1,0:T(8,128)(2,1)S(1)}, u32[]{:S(2)}, u32[]{:S(2)}) collective-permute-start(bf16[24,6144]{1,0:T(8,128)(2,1)S(1)} %get-tuple-element.163), channel_id=1, source_target_pairs={{0,4},{2,6},{4,0},{6,2},{1,5},{3,7},{5,1},{7,3},{8,12},{10,14},{12... | collective-permute-start | bytes 884744 | tf_op jit(solution)/shard_map/ppermute | solution.py:62
  (114 other events, 1439.0 us)
Sparse Core Ops, SparseCore 0:
  30.6 68.1 all-gather.4
  157.9 48.7 all-gather.2
  352.3 53.5 reduce-scatter.4
  428.4 52.4 reduce-scatter.2
